TPU v7x, 32 devices: a whole 2x2x4 slice. The times are simulated.
32 devices in a mesh: lat: 8 (over y, x, core), lon: 4 (over z).
Axes of the slice: x: 2, y: 2, z: 4, core: 2. Of those that a mesh axis runs over, the one named last changes fastest.
Arguments:
- tokens: bfloat16 [2, 96, 96, 512], P(None, 'lat', 'lon'), may hold values from -48 to 48
- region_ids: int32 [2, 96, 96], replicated, may hold values from 0 to 3
- shifts: int32 [2], replicated, may hold values from 1 to 5, as said below
- fine_qkv: bfloat16 [512, 1536], replicated, may hold values from -2 to 2
- fine_proj: bfloat16 [512, 512], replicated, may hold values from -0.25 to 0.25
- merge_weight: bfloat16 [2048, 1024], replicated, may hold values from -0.125 to 0.125
- coarse_qkv: bfloat16 [1024, 1536], replicated, may hold values from -0.1875 to 0.1875
- coarse_proj: bfloat16 [512, 1024], replicated, may hold values from -0.25 to 0.25
Outputs:
- fine_out: bfloat16 [2, 96, 96, 512], P(None, 'lat', 'lon')
- coarse_out: bfloat16 [2, 48, 48, 1024], P(None, 'lat', 'lon')
Inputs may be any that keep to these rules, and one draw needn't show every extreme that they name: `shifts`: entry 0 is the fine level's shift, entry 1 the coarse level's; one of them is 5.
All inputs are finite; a program needn't handle non-finite values.
Results may differ from a plain program's by a relative error of at most 0.012.
The roundings to bfloat16 on the way count: a program that leaves them out, or rounds other values in their place, can miss the bound.
Values may be sent and summed in bfloat16 or wider, within the bound.
No kernel may reach another device: no remote copies, remote signals or barrier semaphores. Data moves between devices by JAX's collectives and lax.ppermute only.
A program may use at most 128 MiB of HBM per device.

v0:
```python
import functools

import jax
import jax.numpy as jnp
import numpy as np
from jax import lax
from jax.experimental import pallas as pl
from jax.experimental.pallas import tpu as pltpu
from jax.sharding import PartitionSpec as P

HD = 32
WH = 6
WW = 12
TOK = 2 * WH * WW
EPS = 1e-05
BIG = 1e30
SCALE = float(np.log2(np.e) / np.sqrt(HD))

NT = (((1,), (1,)), ((), ()))
TN = (((0,), (0,)), ((), ()))
F32 = jnp.float32
BF16 = jnp.bfloat16
I32 = jnp.int32

PAIRS = [(WH - 1, t) for t in range(1, WH)] + [(t, WH - 1) for t in range(1, WH - 1)]


def up16(count):
    return -(-count // 16) * 16


def natural(rows, cols):
    return [(l, r, c) for l in range(2) for r in range(rows) for c in range(cols)]


def windowed(rows, cols):
    return [
        (l, wr * WH + r, wc * WW + c)
        for wr in range(rows // WH)
        for wc in range(cols // WW)
        for l in range(2)
        for r in range(WH)
        for c in range(WW)
    ]


def moved(order, d):
    return [(l, r + d, c + 2 * d) for l, r, c in order]


def exchange_places(held, wanted, rows, cols, sign):
    at = {place: n for n, place in enumerate(held)}
    found = []
    for dr, dc in ((sign, 0), (0, sign), (sign, sign)):
        numbers, places = [], []
        for l, r, c in sorted(set(wanted) - set(held)):
            n = at.get((l, r - dr * rows, c - dc * cols))
            if n is not None:
                numbers.append(n)
                places.append((l, r, c))
        found.append((numbers, places))
    return found


def offsets(t0, t1):
    a = t0 if t0 <= 2 else t0 - WH
    big_a = t1 if t1 <= 2 else t1 - WH
    ahead = 1 if 2 * big_a > a or 2 * big_a - a == 0 and a < 0 else -1
    return a, big_a, ahead


def classes_of(needs, limits):
    which = [next(n for n, limit in enumerate(limits) if need[1] <= limit) for need in needs]
    sizes = [
        [up16(max(need[k] for need, w in zip(needs, which) if w == n)) for k in range(3)]
        for n in range(len(limits))
    ]
    return sizes, which


class Plan:
    def __init__(self, rows, cols):
        crows, ccols = rows // 2, cols // 2
        block, cblock = natural(rows, cols), natural(crows, ccols)
        cases = []
        for t0, t1 in PAIRS:
            a, big_a, ahead = offsets(t0, t1)
            fine = moved(windowed(rows, cols), a)
            coarse = moved(cblock, big_a)
            quarters = [
                (l, 2 * r + dr, 2 * c + dc)
                for dr, dc in ((0, 0), (1, 0), (0, 1), (1, 1))
                for l, r, c in coarse
            ]
            come = 1 if a > 0 else -1
            one = exchange_places(block, fine, rows, cols, come)
            home = [p for p in block if p not in set(fine)]
            wanted = quarters + (home if come == -ahead else [])
            two = exchange_places(fine, wanted, rows, cols, ahead)
            back = 1 if big_a < 0 else -1
            three = exchange_places(coarse, cblock, crows, ccols, back)
            got = set(fine).union(*[places for _, places in two])
            four = exchange_places(fine, [p for p in block if p not in got], rows, cols, back)
            cases.append((come, ahead, back, fine, coarse, quarters, one, two, three, four))

        def needs(which):
            return [[len(numbers) for numbers, _ in case[which]] for case in cases]

        self.one, one_class = classes_of(needs(6), [64, 512])
        self.two, two_class = classes_of(needs(7), [64, 128, 512])
        fine_back = [max(need) > 0 for need in needs(9)]
        self.three = []
        self.four = []
        for with_fine in (False, True):
            inside = [n for n, flag in enumerate(fine_back) if flag == with_fine]
            self.three.append([up16(max(needs(8)[n][k] for n in inside)) for k in range(3)])
            self.four.append([up16(max(needs(9)[n][k] for n in inside)) for k in range(3)])
        three_class = [int(flag) for flag in fine_back]

        def branches(which_class, direction):
            pairs = [(n, case[direction]) for n, case in zip(which_class, cases)]
            found = sorted(set(pairs))
            return found, [found.index(pair) for pair in pairs]

        self.one_branches, one_at = branches(one_class, 0)
        self.two_branches, two_at = branches(two_class, 1)
        self.three_branches, three_at = branches(three_class, 2)
        self.flags = dict(
            one_class=one_class, two_class=two_class, three_class=three_class,
            one_at=one_at, two_at=two_at, three_at=three_at,
            a=[offsets(*pair)[0] for pair in PAIRS], big_a=[offsets(*pair)[1] for pair in PAIRS],
        )

        found = {}
        for n, (come, ahead, back, fine, coarse, quarters, one, two, three, four) in enumerate(cases):

            def send(exchanged, room):
                return [n for (numbers, _), size in zip(exchanged, room) for n in numbers + [-1] * (size - len(numbers))]

            def source(held, *exchanges):
                places = list(held)
                for exchanged, room in exchanges:
                    for (_, got), size in zip(exchanged, room):
                        places += got + [None] * (size - len(got))
                return {p: n for n, p in enumerate(places) if p is not None}

            w = three_class[n]
            first, second = source(block, (one, self.one[-1])), source(fine, (two, self.two[-1]))
            third = source(coarse, (three, self.three[w]))
            last = source(fine, (two, self.two[-1]), (four, self.four[w]))
            out = [(l, r, c) for r in range(crows) for c in range(ccols) for l in range(2)]
            rows_of = dict(
                send_one=send(one, self.one[one_class[n]]),
                take_one=[first[p] for p in fine],
                send_two=send(two, self.two[two_class[n]]),
                take_two=[second[p] for p in quarters],
                send_three=send(three, self.three[w]),
                send_four=send(four, self.four[w]),
                fine_out=[last[p] for p in block],
                coarse_out=[third[p] for p in out],
            )
            for name, row in rows_of.items():
                found.setdefault(name, []).append(row)
        parts, self.at, top = [], {}, 0
        for name, lists in found.items():
            length = -(-max(len(row) for row in lists) // 128)
            part = np.full((len(PAIRS), length * 128), -1, np.float32)
            for n, row in enumerate(lists):
                part[n, : len(row)] = row
            parts.append(part.reshape(len(PAIRS), length, 128))
            self.at[name] = (top, length)
            top += length
        parts.append(np.zeros((len(PAIRS), -top % 8, 128), np.float32))
        self.table = np.concatenate(parts, axis=1)


def case_of(shifts_ref):
    t0, t1 = shifts_ref[0], shifts_ref[1]
    return jnp.where(t0 == WH - 1, t1 - 1, t0 + WH - 2)


def lookup(values, case):
    out = jnp.int32(values[0])
    for n, value in enumerate(values[1:], 1):
        out = jnp.where(case == n, value, out)
    return out


def columns_of(rows, count):
    parts = [jnp.broadcast_to(rows[j : j + 1], (128, 128)).T for j in range(-(-count // 128))]
    return stack_rows(parts)[:count]


def select_rows(index, source):
    lane = lax.broadcasted_iota(I32, (1, 128), 1).astype(F32)
    size = source.shape[0]
    pick = [jnp.where(index == lane + float(at), 1.0, 0.0).astype(BF16) for at in range(0, size, 128)]
    pick = jnp.concatenate(pick, axis=1)[:, :size]
    return jnp.dot(pick, source, preferred_element_type=F32)


def stack_rows(parts):
    return parts[0] if len(parts) == 1 else jnp.concatenate(parts, axis=0)


def layer_norm(values):
    center = jnp.mean(values, axis=-1, keepdims=True)
    values = values - center
    spread = jnp.mean(values * values, axis=-1, keepdims=True)
    return values * lax.rsqrt(spread + EPS)


def attend_windows(qkv_of, id_of, windows, inner, finish):
    lane = lax.broadcasted_iota(I32, (1, 128), 1)
    forbid = jnp.where(lane < 8, BIG, 0.0).astype(BF16)
    groups = inner // 128
    units = [(w, g) for w in range(windows) for g in range(groups)]
    scores, weights, outs = {}, {}, {}

    def score(w, g):
        key_id = id_of(w)
        not_id = (key_id - 1).astype(BF16) * forbid
        q = qkv_of(w, g * 128)
        keys = jnp.concatenate([qkv_of(w, inner + g * 128), key_id], axis=1)
        queries = []
        for h in range(4):
            mine = jnp.where((lane >= h * HD) & (lane < (h + 1) * HD), 1.0, 0.0).astype(BF16)
            queries.append(jnp.concatenate([q * mine, not_id], axis=1))
        scores[w, g] = lax.dot_general(keys, stack_rows(queries), NT, preferred_element_type=F32)

    def soften(w, g):
        s = scores.pop((w, g))
        weight = jnp.exp2((s - jnp.max(s, axis=0, keepdims=True)) * SCALE)
        weights[w, g] = weight.astype(BF16), 1.0 / jnp.sum(weight, axis=0, keepdims=True)

    def gather(w, g):
        weight, scale = weights.pop((w, g))
        out = lax.dot_general(qkv_of(w, 2 * inner + g * 128), weight, TN, preferred_element_type=F32) * scale
        outs[w, g] = [out[h * HD : (h + 1) * HD, h * TOK : (h + 1) * TOK] for h in range(4)]
        if g == groups - 1:
            finish(w, stack_rows([part for k in range(groups) for part in outs.pop((w, k))]).astype(BF16))

    for n in range(len(units) + 2):
        if n < len(units):
            score(*units[n])
        if 0 <= n - 1 < len(units):
            soften(*units[n - 1])
        if 0 <= n - 2 < len(units):
            gather(*units[n - 2])


ANY = pl.BlockSpec(memory_space=pl.ANY)
HBM = pl.BlockSpec(memory_space=pltpu.HBM)
VMEM = pl.BlockSpec(memory_space=pltpu.VMEM)
SMEM = pl.BlockSpec(memory_space=pltpu.SMEM)


def call(body, outs, out_specs, shifts, args, in_specs, scratch, copies, flops, moved_bytes, vmem=32):
    args = [
        pltpu.with_memory_space_constraint(arg, pltpu.HBM) if spec is HBM else arg for arg, spec in zip(args, in_specs)
    ]
    return pl.pallas_call(
        body,
        out_shape=outs,
        in_specs=[SMEM] + in_specs,
        out_specs=out_specs,
        scratch_shapes=list(scratch) + [pltpu.SemaphoreType.DMA((copies,))],
        compiler_params=pltpu.CompilerParams(vmem_limit_bytes=vmem << 20),
        cost_estimate=pl.CostEstimate(flops=flops, bytes_accessed=moved_bytes, transcendentals=0),
    )(shifts, *args)


def shapes(sizes, width, space=pltpu.VMEM):
    return [space((n, width), BF16) for n in sizes]


class Copies:
    def __init__(self, sems):
        self.sems, self.used = sems, 0

    def __call__(self, src, dst):
        copy = pltpu.make_async_copy(src, dst, self.sems.at[self.used])
        self.used += 1
        copy.start()
        return copy


class Pieces:
    def __init__(self, refs, sizes, which, source, own, sems, sem_at):
        self.parts = []
        room = sizes[-1]
        for n, size in enumerate(sizes):
            at, copies, blank = own, [], []
            for k in range(3):
                copies.append((refs[3 * n + k], source.at[pl.ds(at, size[k])], sems.at[sem_at + k]))
                if size[k] < room[k]:
                    blank.append((at + size[k], room[k] - size[k]))
                at += room[k]
            self.parts.append((copies, blank))
        self.which, self.source = which, source
        for n, (copies, blank) in enumerate(self.parts):

            @pl.when(which == n)
            def _():
                for copy in copies:
                    pltpu.make_async_copy(*copy).start()
                for at, rows in blank:
                    source[at : at + rows, :] = jnp.zeros((rows, source.shape[1]), source.dtype)

    def wait(self):
        for n, (copies, _) in enumerate(self.parts):

            @pl.when(self.which == n)
            def _():
                for copy in copies:
                    pltpu.make_async_copy(*copy).wait()


def flat(ref):
    layers, rows, cols, width = ref.shape
    return ref[...].astype(F32).reshape(layers * rows * cols, width).astype(BF16)


def put_pieces(value, refs):
    at = 0
    for ref in refs:
        ref[...] = value[at : at + ref.shape[0]].astype(BF16)
        at += ref.shape[0]


def rows_of(plan, table_ref, name):
    top, length = plan.at[name]
    return table_ref[top : top + length, :]


def send_classes(plan, table_ref, name, source_ref, sizes, which, refs):
    for n, size in enumerate(sizes):

        @pl.when(which == n)
        def _():
            index = columns_of(rows_of(plan, table_ref, name), sum(size))
            put_pieces(select_rows(index, source_ref[...]), refs[3 * n : 3 * n + 3])


def exchange(pieces, sign):
    lat, lon = lax.axis_size("lat"), lax.axis_size("lon")
    row, col, both = pieces
    pairs = [((i + sign) % lat * lon + (j + sign) % lon, i * lon + j) for i in range(lat) for j in range(lon)]
    col = lax.ppermute(col, "lon", [((j + sign) % lon, j) for j in range(lon)])
    both = lax.ppermute(both, ("lat", "lon"), pairs)
    row = lax.ppermute(row, "lat", [((i + sign) % lat, i) for i in range(lat)])
    return [row, col, both]


def unused(like):
    return pl.pallas_call(
        lambda *refs: None,
        out_shape=[jax.ShapeDtypeStruct(x.shape, x.dtype) for x in like],
        out_specs=[ANY] * len(like),
    )()


def choose(index, branches, *args):
    flat_args, tree = jax.tree.flatten(args)
    out_trees = []

    def closed(branch):
        def run(*leaves):
            out, out_tree = jax.tree.flatten(branch(*jax.tree.unflatten(tree, leaves)))
            out_trees.append(out_tree)
            return out

        return jax.make_jaxpr(run)(*flat_args)

    out = lax.cond_p.bind(index, *flat_args, branches=tuple(closed(branch) for branch in branches))
    return jax.tree.unflatten(out_trees[0], out)


def exchange_class(sent, which, sign):
    got = []
    for n in range(len(sent) // 3):
        mine = sent[3 * n : 3 * n + 3]
        got += exchange(mine, sign) if n == which else unused(mine)
    return got


def first_pieces(shifts, tokens, plan):
    width = tokens.shape[-1]
    sizes = plan.one

    def body(shifts_ref, tokens_ref, table_ref, *refs):
        outs, flags = refs[: 3 * len(sizes)], refs[3 * len(sizes) : 3 * len(sizes) + 3]
        held_ref, rows_ref, source_ref, sems = refs[3 * len(sizes) + 3 :]
        case = case_of(shifts_ref)
        start = Copies(sems)
        held = start(tokens_ref, held_ref)
        rows = start(table_ref.at[case], rows_ref)
        for ref, name in zip(flags, ("one_at", "two_at", "three_at")):
            ref[0] = lookup(plan.flags[name], case)
        rows.wait()
        held.wait()
        source_ref[...] = flat(held_ref)
        which = lookup(plan.flags["one_class"], case)
        send_classes(plan, rows_ref, "send_one", source_ref, sizes, which, outs)

    outs = [shape for size in sizes for shape in shapes(size, width)]
    specs = [VMEM] * len(outs) + [SMEM] * 3
    outs += [jax.ShapeDtypeStruct((1,), I32)] * 3
    scratch = [
        pltpu.VMEM(tokens.shape, BF16),
        pltpu.VMEM(plan.table.shape[1:], F32),
        pltpu.VMEM((tokens.size // width, width), BF16),
    ]
    *sent, one, two, three = call(
        body, outs, specs, shifts, [tokens, plan.table], [HBM, HBM], scratch, 2, 1 << 28, 1 << 20
    )
    return sent, one[0], two[0], three[0]


def id_kernel(shifts, regions, plan, rows, cols):
    _, lat, lon = regions.shape
    flat_regions = regions.reshape(2 * lat, lon)
    fine, coarse = windowed(rows, cols), natural(rows // 2, cols // 2)
    places = np.asarray(fine + coarse, np.float32)
    places[len(fine) :, 1:] *= 2
    pad = -len(places) % 128
    places = np.pad(places, ((0, pad), (0, 0))).T.reshape(3, -1, 128)
    is_fine = np.pad(np.ones(len(fine), np.float32), (0, len(coarse) + pad)).reshape(1, -1, 128)
    places = np.concatenate([places, is_fine])
    count = len(fine) + len(coarse)

    def body(shifts_ref, regions_hbm, places_hbm, fine_ref, coarse_ref, regions_ref, places_ref, sems):
        case = case_of(shifts_ref)
        start = Copies(sems)
        waits = [start(regions_hbm, regions_ref), start(places_hbm, places_ref)]
        for copy in waits:
            copy.wait()
        a = lookup(plan.flags["a"], case).astype(F32)
        big_a = 2.0 * lookup(plan.flags["big_a"], case).astype(F32)
        is_fine = places_ref[3]
        d = is_fine * a + (1.0 - is_fine) * big_a
        row = places_ref[1] + d + (lax.axis_index("lat") * rows).astype(F32)
        col = places_ref[2] + 2.0 * d + (lax.axis_index("lon") * cols).astype(F32)
        wrapped = jnp.where((row < 0) | (row >= lat), 4.0, 0.0)
        row = jnp.where(row < 0, row + lat, jnp.where(row >= lat, row - lat, row))
        col = jnp.where(col < 0, col + lon, jnp.where(col >= lon, col - lon, col))
        row = columns_of(row + places_ref[0] * lat, count)
        col = columns_of(col, count)
        wrapped = columns_of(wrapped, count)
        picked = select_rows(row, regions_ref[...].astype(F32).astype(BF16))
        ids = jnp.zeros((count, 128), F32)
        for at in range(0, lon, 128):
            width = min(128, lon - at)
            lane = lax.broadcasted_iota(I32, (1, width), 1).astype(F32) + float(at)
            here = jnp.where(lane == col[:, :width], picked[:, at : at + width], 0.0)
            ids = ids + jnp.sum(here, axis=1, keepdims=True)
        lane = lax.broadcasted_iota(I32, (1, 128), 1).astype(F32)
        hot = jnp.where(lane == ids + wrapped, 1.0, 0.0).astype(BF16)
        fine_ref[...] = hot[: len(fine)]
        coarse_ref[...] = hot[len(fine) :]

    outs = shapes([len(fine), len(coarse)], 128)
    scratch = [pltpu.VMEM(flat_regions.shape, I32), pltpu.VMEM(places.shape, F32)]
    return call(
        body, outs, [VMEM] * 2, shifts, [flat_regions, places], [HBM] * 2, scratch, 2, 1 << 28, 4 << 20
    )


def fine_level(shifts, tokens, pieces, key_id, w_qkv, w_proj, plan):
    _, rows, cols, width = tokens.shape
    count = 2 * rows * cols
    inner = w_proj.shape[0]
    kinds = 3 * len(plan.two)

    def body(shifts_ref, tokens_hbm, *refs):
        piece_refs, refs = refs[: len(pieces)], refs[len(pieces) :]
        id_hbm, qkv_w_hbm, proj_w_hbm, table_ref, out_hbm, *refs = refs
        piece_outs, refs = refs[:kinds], refs[kinds:]
        tokens_ref, source_ref, id_ref, qkv_w_ref, proj_w_ref, rows_ref, x_ref, qkv_ref, out_ref, sems = refs
        case = case_of(shifts_ref)
        start = Copies(sems)
        held = start(tokens_hbm, tokens_ref)
        index = start(table_ref.at[case], rows_ref)
        got = Pieces(piece_refs, plan.one, lookup(plan.flags["one_class"], case), source_ref, count, sems, 12)
        qkv_w, proj_w, ids = start(qkv_w_hbm, qkv_w_ref), start(proj_w_hbm, proj_w_ref), start(id_hbm, id_ref)
        index.wait()
        take = columns_of(rows_of(plan, rows_ref, "take_one"), count)
        held.wait()
        source_ref[:count, :] = flat(tokens_ref)
        got.wait()
        x = select_rows(take, source_ref[...])
        x_ref[...] = x
        normed = layer_norm(x).astype(BF16)
        qkv_w.wait()
        qkv_ref[...] = jnp.dot(normed, qkv_w_ref[...], preferred_element_type=F32).astype(BF16)
        proj_w.wait()
        ids.wait()
        leave = []

        def finish(w, out):
            at = slice(w * TOK, (w + 1) * TOK)
            out = lax.dot_general(out, proj_w_ref[...], TN, preferred_element_type=F32)
            out_ref[at, :] = (x_ref[at, :] + out).astype(BF16)
            leave.append(start(out_ref.at[pl.ds(w * TOK, TOK)], out_hbm.at[pl.ds(w * TOK, TOK)]))

        attend_windows(
            lambda w, at: qkv_ref[w * TOK : (w + 1) * TOK, at : at + 128],
            lambda w: id_ref[w * TOK : (w + 1) * TOK, :],
            count // TOK,
            inner,
            finish,
        )
        which = lookup(plan.flags["two_class"], case)
        send_classes(plan, rows_ref, "send_two", out_ref, plan.two, which, piece_outs)
        for copy in leave:
            copy.wait()

    outs = shapes([count], width, pltpu.HBM) + [shape for size in plan.two for shape in shapes(size, width)]
    specs = [HBM] + [VMEM] * kinds
    scratch = [
        pltpu.VMEM(tokens.shape, BF16),
        pltpu.VMEM((count + sum(plan.one[-1]), width), BF16),
        pltpu.VMEM(key_id.shape, BF16),
        pltpu.VMEM(w_qkv.shape, BF16),
        pltpu.VMEM(w_proj.shape, BF16),
        pltpu.VMEM(plan.table.shape[1:], F32),
        pltpu.VMEM((count, width), F32),
        pltpu.VMEM((count, 3 * inner), BF16),
        pltpu.VMEM((count, width), BF16),
    ]
    args = [tokens, *pieces, key_id, w_qkv, w_proj, plan.table]
    in_specs = [HBM] + [ANY] * (len(pieces) + 1) + [HBM] * 3
    assert 5 + count // TOK <= 16
    out, *sent = call(body, outs, specs, shifts, args, in_specs, scratch, 16, 3 << 30, 6 << 20)
    return out, sent


def coarse_level(shifts, fine, pieces, key_id, w_merge, w_qkv, w_proj, plan):
    count = key_id.shape[0]
    width = w_merge.shape[1]
    own, half = fine.shape
    inner = w_proj.shape[0]
    kinds = 3 * len(plan.three)
    step = w_merge.shape[0] // 4

    def body(shifts_ref, fine_hbm, *refs):
        piece_refs, refs = refs[: len(pieces)], refs[len(pieces) :]
        id_hbm, merge_hbm, qkv_w_hbm, proj_w_hbm, table_ref, out_hbm, *refs = refs
        piece_outs, refs = refs[:kinds], refs[kinds:]
        source_ref, id_ref, merge_ref, qkv_w_ref, proj_w_ref, rows_ref, qkv_ref, out_ref, sems = refs
        case = case_of(shifts_ref)
        start = Copies(sems)
        index = start(table_ref.at[case], rows_ref)
        held = start(fine_hbm, source_ref.at[pl.ds(0, own)])
        got = Pieces(piece_refs, plan.two, lookup(plan.flags["two_class"], case), source_ref, own, sems, 12)
        merge_w = [
            start(merge_hbm.at[pl.ds(n * step, step)], merge_ref.at[pl.ds(n * step, step)]) for n in range(4)
        ]
        qkv_w, proj_w, ids = start(qkv_w_hbm, qkv_w_ref), start(proj_w_hbm, proj_w_ref), start(id_hbm, id_ref)
        index.wait()
        take = columns_of(rows_of(plan, rows_ref, "take_two"), 4 * count)
        held.wait()
        got.wait()
        x = select_rows(take, source_ref[...])
        x = jnp.concatenate([x[n * count : (n + 1) * count] for n in range(4)], axis=1)
        stacked = layer_norm(x).astype(BF16)
        for copy in merge_w:
            copy.wait()
        merged = jnp.dot(stacked, merge_ref[...], preferred_element_type=F32).astype(BF16).astype(F32)
        normed = layer_norm(merged).astype(BF16)
        qkv_w.wait()
        qkv_ref[...] = jnp.dot(normed, qkv_w_ref[...], preferred_element_type=F32).astype(BF16)
        ids.wait()
        proj_w.wait()

        def finish(w, out):
            out = lax.dot_general(out, proj_w_ref[...], TN, preferred_element_type=F32)
            out_ref[...] = (merged + out).astype(BF16)

        attend_windows(lambda w, at: qkv_ref[:, at : at + 128], lambda w: id_ref[...], 1, inner, finish)
        leave = start(out_ref, out_hbm)
        which = lookup(plan.flags["three_class"], case)
        for n, (sizes, fine_sizes) in enumerate(zip(plan.three, plan.four)):

            @pl.when(which == n)
            def _():
                sent = select_rows(columns_of(rows_of(plan, rows_ref, "send_three"), sum(sizes)), out_ref[...])
                sent = sent.astype(BF16)
                at = 0
                for ref, size in zip(piece_outs[3 * n :], sizes):
                    ref[:size, :] = sent[at : at + size, :half]
                    ref[size : 2 * size, :] = sent[at : at + size, half:]
                    at += size
                if sum(fine_sizes):
                    index = columns_of(rows_of(plan, rows_ref, "send_four"), sum(fine_sizes))
                    sent = select_rows(index, source_ref[:own, :]).astype(BF16)
                    at = 0
                    for ref, size, more in zip(piece_outs[3 * n :], sizes, fine_sizes):
                        ref[2 * size :, :] = sent[at : at + more]
                        at += more

        leave.wait()

    outs = shapes([count], width, pltpu.HBM)
    for sizes, fine_sizes in zip(plan.three, plan.four):
        outs += shapes([2 * n + m for n, m in zip(sizes, fine_sizes)], half)
    specs = [HBM] + [VMEM] * kinds
    scratch = [
        pltpu.VMEM((own + sum(plan.two[-1]), half), BF16),
        pltpu.VMEM(key_id.shape, BF16),
        pltpu.VMEM(w_merge.shape, BF16),
        pltpu.VMEM(w_qkv.shape, BF16),
        pltpu.VMEM(w_proj.shape, BF16),
        pltpu.VMEM(plan.table.shape[1:], F32),
        pltpu.VMEM((count, 3 * inner), BF16),
        pltpu.VMEM((count, width), BF16),
    ]
    args = [fine, *pieces, key_id, w_merge, w_qkv, w_proj, plan.table]
    in_specs = [HBM] + [ANY] * (len(pieces) + 1) + [HBM] * 4
    out, *sent = call(body, outs, specs, shifts, args, in_specs, scratch, 16, 3 << 30, 12 << 20)
    return out, sent


def fine_output(shifts, fine, pieces, got, which, plan, rows, cols):
    own, width = fine.shape
    room = sum(plan.two[-1])
    extra = plan.four[which]

    def body(shifts_ref, fine_hbm, *refs):
        piece_refs, refs = refs[: len(pieces)], refs[len(pieces) :]
        got_refs, refs = refs[: len(got)], refs[len(got) :]
        table_ref, out_ref, source_ref, rows_ref, sems = refs
        case = case_of(shifts_ref)
        start = Copies(sems)
        waits = [start(table_ref.at[case], rows_ref), start(fine_hbm, source_ref.at[pl.ds(0, own)])]
        at = own + room
        for ref, size, more in zip(got_refs, plan.three[which], extra):
            waits.append(start(ref.at[pl.ds(2 * size, more)], source_ref.at[pl.ds(at, more)]))
            at += more
        pieces_in = Pieces(piece_refs, plan.two, lookup(plan.flags["two_class"], case), source_ref, own, sems, 8)
        for copy in waits:
            copy.wait()
        take = columns_of(rows_of(plan, rows_ref, "fine_out"), own)
        pieces_in.wait()
        out = select_rows(take, source_ref[...])
        out_ref[...] = out.reshape(2, rows, cols, width).astype(BF16)

    outs = [jax.ShapeDtypeStruct((2, rows, cols, width), BF16)]
    scratch = [
        pltpu.VMEM((own + room + (sum(extra) if got else 0), width), BF16),
        pltpu.VMEM(plan.table.shape[1:], F32),
    ]
    args = [fine, *pieces, *got, plan.table]
    in_specs = [HBM] + [ANY] * (len(pieces) + len(got)) + [HBM]
    return call(body, outs, [VMEM], shifts, args, in_specs, scratch, 16, 1 << 30, 4 << 20)[0]


def coarse_output(shifts, coarse, got, which, plan, rows, cols):
    own, width = coarse.shape
    half = width // 2
    sizes = plan.three[which]

    def body(shifts_ref, coarse_hbm, *refs):
        got_refs, (table_ref, out_ref, source_ref, rows_ref, sems) = refs[:3], refs[3:]
        start = Copies(sems)
        waits = [start(table_ref.at[case_of(shifts_ref)], rows_ref), start(coarse_hbm, source_ref.at[pl.ds(0, own)])]
        at = own
        for ref, size in zip(got_refs, sizes):
            for n in range(2):
                to = source_ref.at[pl.ds(at, size), pl.ds(n * half, half)]
                waits.append(start(ref.at[pl.ds(n * size, size)], to))
            at += size
        for copy in waits:
            copy.wait()
        take = columns_of(rows_of(plan, rows_ref, "coarse_out"), own)
        out = select_rows(take, source_ref[...]).astype(BF16)
        for n in range(own // 2):
            out_ref[n // cols, n % cols] = out[2 * n : 2 * n + 2]

    outs = [jax.ShapeDtypeStruct((rows, cols, 2, width), BF16)]
    scratch = [pltpu.VMEM((own + sum(sizes), width), BF16), pltpu.VMEM(plan.table.shape[1:], F32)]
    args = [coarse, *got, plan.table]
    out = call(body, outs, [VMEM], shifts, args, [HBM] + [ANY] * 3 + [HBM], scratch, 8, 1 << 28, 1 << 20)[0]
    return out.transpose(2, 0, 1, 3)


def on_device(tokens, regions, shifts, fine_qkv, fine_proj, merge_weight, coarse_qkv, coarse_proj):
    _, rows, cols, _ = tokens.shape
    plan = Plan(rows, cols)

    def first(which, sign, sent, shifts, regions):
        got = exchange_class(sent, which, sign)
        return got, id_kernel(shifts, regions, plan, rows, cols)

    def second(which, sign, sent):
        return exchange_class(sent, which, sign)

    def third(which, sign, sent, shifts, fine, pieces, coarse):
        got = exchange(sent[3 * which : 3 * which + 3], sign)
        fine_out = fine_output(shifts, fine, pieces, got if which else [], which, plan, rows, cols)
        return fine_out, coarse_output(shifts, coarse, got, which, plan, rows // 2, cols // 2)

    def branches(stage, pairs):
        return [functools.partial(stage, which, sign) for which, sign in pairs]

    sent, one, two, three = first_pieces(shifts, tokens, plan)
    got, (fine_id, coarse_id) = choose(one, branches(first, plan.one_branches), sent, shifts, regions)
    fine, sent = fine_level(shifts, tokens, got, fine_id, fine_qkv, fine_proj, plan)
    got = choose(two, branches(second, plan.two_branches), sent)
    coarse, sent = coarse_level(
        shifts, fine, got, coarse_id, merge_weight, coarse_qkv, coarse_proj, plan
    )
    return choose(three, branches(third, plan.three_branches), sent, shifts, fine, got, coarse)


def solution(mesh):
    return jax.shard_map(
        on_device,
        mesh=mesh,
        in_specs=(P(None, "lat", "lon", None), P(), P(), P(), P(), P(), P(), P()),
        out_specs=(P(None, "lat", "lon", None), P(None, "lat", "lon", None)),
        check_vma=False,
    )
```

profile of v0, /device:TPU:0, one launch (start us, length us, event | category | flops | bytes accessed | tf_op | source)
XLA Modules:
  0.0 52.0 jit_solution(9697391063812405124)
XLA Ops:
  0.6 2.8 %shard_map.110 = (bf16[48,512]{1,0:T(8,128)(2,1)S(1)}, bf16[48,512]{1,0:T(8,128)(2,1)S(1)}, bf16[16,512]{1,0:T(8,128)(2,1)S(1)}, bf16[112,512]{1,0:T(8,128)(2,1)...) custom-call(s32[2]{0:T(128)} %shifts_ref.5, ...), custom_call_target="tpu_custom_call" | custom-call | flops 268435456 | bytes 1048576 | tf_op jit(solution)/shard_map/pallas_call | solution.py:262
  3.4 12.4 %conditional.3 = (bf16[48,512]{1,0:T(8,128)(2,1)}, bf16[48,512]{1,0:T(8,128)(2,1)}, bf16[16,512]{1,0:T(8,128)(2,1)}, bf16[112,512]{1,0:T(8,128)(2,1)}, bf16[112,...) conditional(s32[]{:T(128)} %bitcast.8, ...), branch_computations={%region_0.0_spmd, %region_1.0_spmd, %region_2.0_spmd, %region_3.0_... | conditional | flops 268435456 | bytes 5308600 | solution.py:375
  4.1 0.5 collective-permute-start.6
  4.6 2.6 %collective-permute-start.7 = (bf16[112,512]{1,0:T(8,128)(2,1)S(1)}, bf16[112,512]{1,0:T(8,128)(2,1)}, u32[]{:S(2)}, u32[]{:S(2)}) collective-permute-start(bf16[112,512]{1,0:T(8,128)(2,1)S(1)} %get-tuple-element.184), channel_id=1, source_target_pairs={{3,0},{0,1},{1,2},{2,3},{7,4},{4,5},{5,6},{6,7},{11,8},{8,9},{9,10... | collective-permute-start | bytes 344072 | tf_op jit(solution)/shard_map/cond/branch_2_fun/ppermute | solution.py:349
  7.2 2.4 %collective-permute-start.8 = (bf16[48,512]{1,0:T(8,128)(2,1)S(1)}, bf16[48,512]{1,0:T(8,128)(2,1)}, u32[]{:S(2)}, u32[]{:S(2)}) collective-permute-start(bf16[48,512]{1,0:T(8,128)(2,1)S(1)} %get-tuple-element.185), channel_id=1, source_target_pairs={{31,0},{28,1},{29,2},{30,3},{3,4},{0,5},{1,6},{2,7},{7,8},{4,9},{5... | collective-permute-start | bytes 147464 | tf_op jit(solution)/shard_map/cond/branch_2_fun/ppermute | solution.py:350
  9.6 2.1 %branch_2_fun.7 = (bf16[576,128]{1,0:T(8,128)(2,1)S(1)}, bf16[144,128]{1,0:T(8,128)(2,1)S(1)}) custom-call(s32[2]{0:T(128)} %get-tuple-element.186.shifts_ref, s32[192,96]{1,0:T(8,128)} %bitcast.12, f32[4,6,128]{2,1,0:T(8,128)} %constant.5.clone.places_hbm), custom_call_target="tpu_custom_call" | custom-call | flops 268435456 | bytes 4194304 | tf_op jit(solution)/shard_map/cond/branch_2_fun/pallas_call | solution.py:262
  11.8 4.1 %collective-permute-done.8 = bf16[48,512]{1,0:T(8,128)(2,1)} collective-permute-done((bf16[48,512]{1,0:T(8,128)(2,1)S(1)}, bf16[48,512]{1,0:T(8,128)(2,1)}, u32[]{:S(2)}, u32[]{:S(2)}) %collective-permute-start.8) | collective-permute-done | bytes 49184 | tf_op jit(solution)/shard_map/cond/branch_2_fun/ppermute | solution.py:350
  15.8 0.0 collective-permute-done.6
  15.8 0.0 collective-permute-done.7
  15.8 0.0 copy-start
  15.8 8.8 %shard_map.111 = (bf16[576,512]{1,0:T(8,128)(2,1)}, bf16[48,512]{1,0:T(8,128)(2,1)S(1)}, bf16[48,512]{1,0:T(8,128)(2,1)S(1)}, bf16[16,512]{1,0:T(8,128)(2,1)S(1)...) custom-call(s32[2]{0:T(128)} %shifts_ref.5, ...), custom_call_target="tpu_custom_call" | custom-call | flops 3221225472 | bytes 6291456 | tf_op jit(solution)/shard_map/pallas_call | solution.py:262
  24.6 7.3 %conditional.4 = (bf16[48,512]{1,0:T(8,128)(2,1)S(1)}, bf16[48,512]{1,0:T(8,128)(2,1)S(1)}, bf16[16,512]{1,0:T(8,128)(2,1)S(1)}, bf16[128,512]{1,0:T(8,128)(2,1)...) conditional(s32[]{:T(128)} %bitcast.9, ...), branch_computations={%region_4.0_spmd, %region_5.0_spmd, %region_6.0_spmd, %region_7.0_... | conditional | bytes 1769664 | solution.py:375
  25.3 0.6 %collective-permute-start.18 = (bf16[128,512]{1,0:T(8,128)(2,1)S(1)}, bf16[128,512]{1,0:T(8,128)(2,1)}, u32[]{:S(2)}, u32[]{:S(2)}) collective-permute-start(bf16[128,512]{1,0:T(8,128)(2,1)S(1)} %get-tuple-element.221), channel_id=1, source_target_pairs={{4,0},{8,4},{12,8},{16,12},{20,16},{24,20},{28,24},{0,28},{5,1},{9... | collective-permute-start | bytes 393224 | tf_op jit(solution)/shard_map/cond/branch_2_fun/ppermute | solution.py:351
  25.9 1.7 %collective-permute-start.19 = (bf16[128,512]{1,0:T(8,128)(2,1)S(1)}, bf16[128,512]{1,0:T(8,128)(2,1)}, u32[]{:S(2)}, u32[]{:S(2)}) collective-permute-start(bf16[128,512]{1,0:T(8,128)(2,1)S(1)} %get-tuple-element.222), channel_id=1, source_target_pairs={{1,0},{2,1},{3,2},{0,3},{5,4},{6,5},{7,6},{4,7},{9,8},{10,9},{11,1... | collective-permute-start | bytes 393224 | tf_op jit(solution)/shard_map/cond/branch_2_fun/ppermute | solution.py:349
  27.7 0.4 collective-permute-start.20
  28.1 3.8 %collective-permute-done.20 = bf16[48,512]{1,0:T(8,128)(2,1)} collective-permute-done((bf16[48,512]{1,0:T(8,128)(2,1)S(1)}, bf16[48,512]{1,0:T(8,128)(2,1)}, u32[]{:S(2)}, u32[]{:S(2)}) %collective-permute-start.20) | collective-permute-done | bytes 49184 | tf_op jit(solution)/shard_map/cond/branch_2_fun/ppermute | solution.py:350
  31.9 0.0 collective-permute-done.18
  31.9 0.1 collective-permute-done.19
  31.9 0.0 copy-done
  31.9 6.8 %shard_map.112 = (bf16[144,1024]{1,0:T(8,128)(2,1)}, bf16[64,512]{1,0:T(8,128)(2,1)S(1)}, bf16[64,512]{1,0:T(8,128)(2,1)S(1)}, bf16[32,512]{1,0:T(8,128)(2,1)S(1...) custom-call(s32[2]{0:T(128)S(1)} %copy-done, ...), custom_call_target="tpu_custom_call" | custom-call | flops 3221225472 | bytes 12582912 | tf_op jit(solution)/shard_map/pallas_call | solution.py:262
  38.7 13.1 %conditional.5 = (bf16[2,12,24,512]{3,2,1,0:T(8,128)(2,1)}, bf16[2,6,12,1024]{3,0,2,1:T(2,128)(2,1)}) conditional(s32[]{:T(128)} %bitcast.7, (s32[2]{0:T(128)S(1)}, bf16[576,512]{1,0:T(8,128)(2,1)}, bf16[48,512]{1,0:T(8,128)(2,1)S(1)}, bf16[48,512]{1,0:T(8,128)(2,1)S(1)}, bf16[16,512]{1,0:T(8,128)(2,1)S(1)}, ...), branch_computations={%region_9.0_spmd, %region_10.0_spmd, %region_11.0_spmd} | conditional | flops 1342177280 | bytes 6881416 | solution.py:375
  39.4 5.3 %collective-permute-start.32 = (bf16[32,512]{1,0:T(8,128)(2,1)S(1)}, bf16[32,512]{1,0:T(8,128)(2,1)S(1)}, u32[]{:S(2)}, u32[]{:S(2)}) collective-permute-start(bf16[32,512]{1,0:T(8,128)(2,1)S(1)} %get-tuple-element.274), channel_id=1, source_target_pairs={{5,0},{6,1},{7,2},{4,3},{9,4},{10,5},{11,6},{8,7},{13,8},{14,9},{1... | collective-permute-start | bytes 98312 | tf_op jit(solution)/shard_map/cond/branch_1_fun/ppermute | solution.py:350
  44.7 0.0 collective-permute-start.30
  44.7 0.6 %collective-permute-start.31 = (bf16[64,512]{1,0:T(8,128)(2,1)S(1)}, bf16[64,512]{1,0:T(8,128)(2,1)S(1)}, u32[]{:S(2)}, u32[]{:S(2)}) collective-permute-start(bf16[64,512]{1,0:T(8,128)(2,1)S(1)} %get-tuple-element.273), channel_id=1, source_target_pairs={{1,0},{2,1},{3,2},{0,3},{5,4},{6,5},{7,6},{4,7},{9,8},{10,9},{11,1... | collective-permute-start | bytes 196616 | tf_op jit(solution)/shard_map/cond/branch_1_fun/ppermute | solution.py:349
  45.3 3.5 %branch_1_fun.10 = bf16[2,12,24,512]{3,2,1,0:T(8,128)(2,1)} custom-call(s32[2]{0:T(128)S(1)} %get-tuple-element.260.shifts_ref, bf16[576,512]{1,0:T(8,128)(2,1)} %get-tuple-element.261.fine_hbm, bf16[48,512]{1,0:T(8,128)(2,1)S(1)} %get-tuple-element.262.refs_0_, bf16[48,512]{1,0:T(8,128)(2,1)S(1)} %get-tuple-element.263.refs_1_, ...), custom_call_target="tpu_custom_call" | custom-call | flops 1073741824 | bytes 4194304 | tf_op jit(solution)/shard_map/cond/branch_1_fun/pallas_call | solution.py:262
  48.9 0.0 collective-permute-done.32.refs_2_
  48.9 0.0 collective-permute-done.30.refs_0_
  48.9 0.3 collective-permute-done.31.refs_1_
  49.2 2.6 %branch_1_fun.11 = bf16[6,12,2,1024]{3,2,1,0:T(2,128)(2,1)} custom-call(s32[2]{0:T(128)S(1)} %get-tuple-element.260.shifts_ref, bf16[144,1024]{1,0:T(8,128)(2,1)} %get-tuple-element.271.coarse_hbm, bf16[64,512]{1,0:T(8,128)(2,1)S(1)} %collective-permute-done.30.refs_0_, bf16[64,512]{1,0:T(8,128)(2,1)S(1)} %collective-permute-done.31.refs_1_, ...), custom_call_target="tpu_custom_call" | custom-call | flops 268435456 | bytes 1048576 | tf_op jit(solution)/shard_map/cond/branch_1_fun/pallas_call | solution.py:262
  (3 shorter events, 0.0 us)
Async XLA Ops:
  4.1 11.8 %collective-permute-start.6 = (bf16[112,512]{1,0:T(8,128)(2,1)S(1)}, bf16[112,512]{1,0:T(8,128)(2,1)}, u32[]{:S(2)}, u32[]{:S(2)}) collective-permute-start(bf16[112,512]{1,0:T(8,128)(2,1)S(1)} %get-tuple-element.183), channel_id=1, source_target_pairs={{28,0},{0,4},{4,8},{8,12},{12,16},{16,20},{20,24},{24,28},{29,1},{... | collective-permute-start | bytes 344072 | tf_op jit(solution)/shard_map/cond/branch_2_fun/ppermute | solution.py:351
  4.6 11.2 %collective-permute-start.7 = (bf16[112,512]{1,0:T(8,128)(2,1)S(1)}, bf16[112,512]{1,0:T(8,128)(2,1)}, u32[]{:S(2)}, u32[]{:S(2)}) collective-permute-start(bf16[112,512]{1,0:T(8,128)(2,1)S(1)} %get-tuple-element.184), channel_id=1, source_target_pairs={{3,0},{0,1},{1,2},{2,3},{7,4},{4,5},{5,6},{6,7},{11,8},{8,9},{9,10... | collective-permute-start | bytes 344072 | tf_op jit(solution)/shard_map/cond/branch_2_fun/ppermute | solution.py:349
  7.2 8.6 %collective-permute-start.8 = (bf16[48,512]{1,0:T(8,128)(2,1)S(1)}, bf16[48,512]{1,0:T(8,128)(2,1)}, u32[]{:S(2)}, u32[]{:S(2)}) collective-permute-start(bf16[48,512]{1,0:T(8,128)(2,1)S(1)} %get-tuple-element.185), channel_id=1, source_target_pairs={{31,0},{28,1},{29,2},{30,3},{3,4},{0,5},{1,6},{2,7},{7,8},{4,9},{5... | collective-permute-start | bytes 147464 | tf_op jit(solution)/shard_map/cond/branch_2_fun/ppermute | solution.py:350
  15.8 16.1 %copy-start = (s32[2]{0:T(128)S(1)}, s32[2]{0:T(128)}, u32[]{:S(2)}) copy-start(s32[2]{0:T(128)} %shifts_ref.5) | copy-start | bytes 28
  25.3 6.5 %collective-permute-start.18 = (bf16[128,512]{1,0:T(8,128)(2,1)S(1)}, bf16[128,512]{1,0:T(8,128)(2,1)}, u32[]{:S(2)}, u32[]{:S(2)}) collective-permute-start(bf16[128,512]{1,0:T(8,128)(2,1)S(1)} %get-tuple-element.221), channel_id=1, source_target_pairs={{4,0},{8,4},{12,8},{16,12},{20,16},{24,20},{28,24},{0,28},{5,1},{9... | collective-permute-start | bytes 393224 | tf_op jit(solution)/shard_map/cond/branch_2_fun/ppermute | solution.py:351
  25.9 6.0 %collective-permute-start.19 = (bf16[128,512]{1,0:T(8,128)(2,1)S(1)}, bf16[128,512]{1,0:T(8,128)(2,1)}, u32[]{:S(2)}, u32[]{:S(2)}) collective-permute-start(bf16[128,512]{1,0:T(8,128)(2,1)S(1)} %get-tuple-element.222), channel_id=1, source_target_pairs={{1,0},{2,1},{3,2},{0,3},{5,4},{6,5},{7,6},{4,7},{9,8},{10,9},{11,1... | collective-permute-start | bytes 393224 | tf_op jit(solution)/shard_map/cond/branch_2_fun/ppermute | solution.py:349
  27.7 4.2 %collective-permute-start.20 = (bf16[48,512]{1,0:T(8,128)(2,1)S(1)}, bf16[48,512]{1,0:T(8,128)(2,1)}, u32[]{:S(2)}, u32[]{:S(2)}) collective-permute-start(bf16[48,512]{1,0:T(8,128)(2,1)S(1)} %get-tuple-element.223), channel_id=1, source_target_pairs={{5,0},{6,1},{7,2},{4,3},{9,4},{10,5},{11,6},{8,7},{13,8},{14,9},{1... | collective-permute-start | bytes 147464 | tf_op jit(solution)/shard_map/cond/branch_2_fun/ppermute | solution.py:350
  39.4 9.4 %collective-permute-start.32 = (bf16[32,512]{1,0:T(8,128)(2,1)S(1)}, bf16[32,512]{1,0:T(8,128)(2,1)S(1)}, u32[]{:S(2)}, u32[]{:S(2)}) collective-permute-start(bf16[32,512]{1,0:T(8,128)(2,1)S(1)} %get-tuple-element.274), channel_id=1, source_target_pairs={{5,0},{6,1},{7,2},{4,3},{9,4},{10,5},{11,6},{8,7},{13,8},{14,9},{1... | collective-permute-start | bytes 98312 | tf_op jit(solution)/shard_map/cond/branch_1_fun/ppermute | solution.py:350
  44.7 4.2 %collective-permute-start.30 = (bf16[64,512]{1,0:T(8,128)(2,1)S(1)}, bf16[64,512]{1,0:T(8,128)(2,1)S(1)}, u32[]{:S(2)}, u32[]{:S(2)}) collective-permute-start(bf16[64,512]{1,0:T(8,128)(2,1)S(1)} %get-tuple-element.272), channel_id=1, source_target_pairs={{4,0},{8,4},{12,8},{16,12},{20,16},{24,20},{28,24},{0,28},{5,1},{9... | collective-permute-start | bytes 196616 | tf_op jit(solution)/shard_map/cond/branch_1_fun/ppermute | solution.py:351
  44.7 4.5 %collective-permute-start.31 = (bf16[64,512]{1,0:T(8,128)(2,1)S(1)}, bf16[64,512]{1,0:T(8,128)(2,1)S(1)}, u32[]{:S(2)}, u32[]{:S(2)}) collective-permute-start(bf16[64,512]{1,0:T(8,128)(2,1)S(1)} %get-tuple-element.273), channel_id=1, source_target_pairs={{1,0},{2,1},{3,2},{0,3},{5,4},{6,5},{7,6},{4,7},{9,8},{10,9},{11,1... | collective-permute-start | bytes 196616 | tf_op jit(solution)/shard_map/cond/branch_1_fun/ppermute | solution.py:349
where the time goes:
time: 52.6 us; the launch traced here: 52 us
  Pallas kernels  26.6 us (51%)
  starting transfers between devices  14.2 us (27%)
  waiting for transfers between devices  8.25 us (16%)
  loops' own time  2.09 us (4%)
  between operations  0.82 us (2%)
    pallas_call x6, Pallas kernels, call(): pl.pallas_call(body, out_shape=outs, in_specs=[SMEM] + in_specs, out_spec...  26.6 us
    ppermute x3, starting transfers between devices, exchange(): both = lax.ppermute(both, ('lat', 'lon'), pairs)  8.09 us
    ppermute x3, waiting for transfers between devices, exchange(): both = lax.ppermute(both, ('lat', 'lon'), pairs)  7.86 us
    ppermute x3, starting transfers between devices, exchange(): col = lax.ppermute(col, 'lon', [((j + sign) % lon, j) for j in range(lon)])  5.01 us
    another operation x3, loops' own time, choose(): lax.cond_p.bind(index, *flat_args, branches=tuple((closed(branch) for bra...  2.09 us
    ppermute x3, starting transfers between devices, exchange(): row = lax.ppermute(row, 'lat', [((i + sign) % lat, i) for i in range(lat)])  1.14 us
  transfers between devices with their start and end apart: 9, of which 4 were waited for; matrix products, arithmetic and copies ran while one was open for 0% of the time, Pallas kernels for 11%

commit v1 on v0

--- a/solution.py
+++ b/solution.py
@@ -255,19 +255,21 @@
 SMEM = pl.BlockSpec(memory_space=pltpu.SMEM)
 
 
-def call(body, outs, out_specs, shifts, args, in_specs, scratch, copies, flops, moved_bytes, vmem=32):
+def call(body, outs, args, in_specs, scratch, copies, flops, moved_bytes, vmem=32):
     args = [
-        pltpu.with_memory_space_constraint(arg, pltpu.HBM) if spec is HBM else arg for arg, spec in zip(args, in_specs)
+        pltpu.with_memory_space_constraint(arg, spec.memory_space) for arg, spec in zip(args, in_specs, strict=True)
     ]
+    spaces = [getattr(out, "memory_space", pltpu.SMEM if out.dtype == I32 else pltpu.VMEM) for out in outs]
+    out_specs = [pl.BlockSpec(memory_space=space) for space in spaces]
     return pl.pallas_call(
         body,
         out_shape=outs,
-        in_specs=[SMEM] + in_specs,
+        in_specs=in_specs,
         out_specs=out_specs,
         scratch_shapes=list(scratch) + [pltpu.SemaphoreType.DMA((copies,))],
         compiler_params=pltpu.CompilerParams(vmem_limit_bytes=vmem << 20),
         cost_estimate=pl.CostEstimate(flops=flops, bytes_accessed=moved_bytes, transcendentals=0),
-    )(shifts, *args)
+    )(*args)
 
 
 def shapes(sizes, width, space=pltpu.VMEM):
@@ -285,35 +287,17 @@
         return copy
 
 
-class Pieces:
-    def __init__(self, refs, sizes, which, source, own, sems, sem_at):
-        self.parts = []
-        room = sizes[-1]
-        for n, size in enumerate(sizes):
-            at, copies, blank = own, [], []
-            for k in range(3):
-                copies.append((refs[3 * n + k], source.at[pl.ds(at, size[k])], sems.at[sem_at + k]))
-                if size[k] < room[k]:
-                    blank.append((at + size[k], room[k] - size[k]))
-                at += room[k]
-            self.parts.append((copies, blank))
-        self.which, self.source = which, source
-        for n, (copies, blank) in enumerate(self.parts):
-
-            @pl.when(which == n)
-            def _():
-                for copy in copies:
-                    pltpu.make_async_copy(*copy).start()
-                for at, rows in blank:
-                    source[at : at + rows, :] = jnp.zeros((rows, source.shape[1]), source.dtype)
-
-    def wait(self):
-        for n, (copies, _) in enumerate(self.parts):
-
-            @pl.when(self.which == n)
-            def _():
-                for copy in copies:
-                    pltpu.make_async_copy(*copy).wait()
+def lay_pieces(refs, sizes, which, source):
+    for n, size in enumerate(sizes):
+
+        @pl.when(which == n)
+        def _():
+            at = 0
+            for ref, rows, room in zip(refs[3 * n : 3 * n + 3], size, sizes[-1]):
+                source[at : at + rows, :] = ref[...]
+                if rows < room:
+                    source[at + rows : at + room, :] = jnp.zeros((room - rows, source.shape[1]), source.dtype)
+                at += room
 
 
 def flat(ref):
@@ -328,18 +312,17 @@
         at += ref.shape[0]
 
 
-def rows_of(plan, table_ref, name):
+def rows_of(plan, table_ref, name, *lead):
     top, length = plan.at[name]
-    return table_ref[top : top + length, :]
-
-
-def send_classes(plan, table_ref, name, source_ref, sizes, which, refs):
+    return table_ref[(*lead, slice(top, top + length), slice(None))]
+
+
+def send_classes(plan, rows, source_ref, sizes, which, refs):
     for n, size in enumerate(sizes):
 
         @pl.when(which == n)
         def _():
-            index = columns_of(rows_of(plan, table_ref, name), sum(size))
-            put_pieces(select_rows(index, source_ref[...]), refs[3 * n : 3 * n + 3])
+            put_pieces(select_rows(columns_of(rows, sum(size)), source_ref[...]), refs[3 * n : 3 * n + 3])
 
 
 def exchange(pieces, sign):
@@ -353,10 +336,9 @@
 
 
 def unused(like):
+    outs = [pltpu.VMEM(x.shape, x.dtype) for x in like]
     return pl.pallas_call(
-        lambda *refs: None,
-        out_shape=[jax.ShapeDtypeStruct(x.shape, x.dtype) for x in like],
-        out_specs=[ANY] * len(like),
+        lambda *refs: None, out_shape=outs, out_specs=[pl.BlockSpec(memory_space=pltpu.VMEM)] * len(outs)
     )()
 
 
@@ -384,40 +366,45 @@
     return got
 
 
+FLAGS = ("one_class", "two_class", "three_class", "a", "big_a")
+
+
 def first_pieces(shifts, tokens, plan):
     width = tokens.shape[-1]
+    count = tokens.size // width
     sizes = plan.one
-
-    def body(shifts_ref, tokens_ref, table_ref, *refs):
-        outs, flags = refs[: 3 * len(sizes)], refs[3 * len(sizes) : 3 * len(sizes) + 3]
-        held_ref, rows_ref, source_ref, sems = refs[3 * len(sizes) + 3 :]
+    kinds = 3 * len(sizes)
+
+    def body(shifts_hbm, tokens_hbm, table_hbm, *refs):
+        outs, refs = refs[:kinds], refs[kinds:]
+        source_ref, rows_ref, flags_ref, *at_refs, shifts_ref, tokens_ref, table_ref, sems = refs
+        start = Copies(sems)
+        shift = start(shifts_hbm, shifts_ref)
+        held = start(tokens_hbm, tokens_ref)
+        table = start(table_hbm, table_ref)
+        shift.wait()
         case = case_of(shifts_ref)
-        start = Copies(sems)
-        held = start(tokens_ref, held_ref)
-        rows = start(table_ref.at[case], rows_ref)
-        for ref, name in zip(flags, ("one_at", "two_at", "three_at")):
+        for ref, name in zip(at_refs, ("one_at", "two_at", "three_at")):
             ref[0] = lookup(plan.flags[name], case)
-        rows.wait()
+        for n, name in enumerate(FLAGS):
+            flags_ref[n] = lookup(plan.flags[name], case)
+        which = lookup(plan.flags["one_class"], case)
         held.wait()
-        source_ref[...] = flat(held_ref)
-        which = lookup(plan.flags["one_class"], case)
-        send_classes(plan, rows_ref, "send_one", source_ref, sizes, which, outs)
-
-    outs = [shape for size in sizes for shape in shapes(size, width)]
-    specs = [VMEM] * len(outs) + [SMEM] * 3
+        source_ref[...] = flat(tokens_ref)
+        table.wait()
+        rows_ref[...] = table_ref[case]
+        send_classes(plan, rows_of(plan, table_ref, "send_one", case), source_ref, sizes, which, outs)
+
+    outs = [shape for size in sizes for shape in shapes(size, width)] + shapes([count], width)
+    outs += [pltpu.VMEM(plan.table.shape[1:], F32), pltpu.SMEM((8,), I32)]
     outs += [jax.ShapeDtypeStruct((1,), I32)] * 3
-    scratch = [
-        pltpu.VMEM(tokens.shape, BF16),
-        pltpu.VMEM(plan.table.shape[1:], F32),
-        pltpu.VMEM((tokens.size // width, width), BF16),
-    ]
-    *sent, one, two, three = call(
-        body, outs, specs, shifts, [tokens, plan.table], [HBM, HBM], scratch, 2, 1 << 28, 1 << 20
-    )
-    return sent, one[0], two[0], three[0]
-
-
-def id_kernel(shifts, regions, plan, rows, cols):
+    scratch = [pltpu.SMEM((2,), I32), pltpu.VMEM(tokens.shape, BF16), pltpu.VMEM(plan.table.shape, F32)]
+    got = call(body, outs, [shifts, tokens, plan.table], [HBM] * 3, scratch, 3, 1 << 28, 1 << 20)
+    sent, (source, rows, flags, one, two, three) = got[:kinds], got[kinds:]
+    return sent, source, rows, flags, one[0], two[0], three[0]
+
+
+def id_kernel(flags, regions, weights, plan, rows, cols):
     _, lat, lon = regions.shape
     flat_regions = regions.reshape(2 * lat, lon)
     fine, coarse = windowed(rows, cols), natural(rows // 2, cols // 2)
@@ -429,14 +416,17 @@
     places = np.concatenate([places, is_fine])
     count = len(fine) + len(coarse)
 
-    def body(shifts_ref, regions_hbm, places_hbm, fine_ref, coarse_ref, regions_ref, places_ref, sems):
-        case = case_of(shifts_ref)
+    def body(flags_ref, regions_hbm, places_hbm, *refs):
+        weights_hbm, refs = refs[: len(weights)], refs[len(weights) :]
+        fine_ref, coarse_ref, *refs = refs
+        weight_refs, (regions_ref, places_ref, sems) = refs[: len(weights)], refs[len(weights) :]
         start = Copies(sems)
         waits = [start(regions_hbm, regions_ref), start(places_hbm, places_ref)]
+        later = [start(src, dst) for src, dst in zip(weights_hbm, weight_refs)]
         for copy in waits:
             copy.wait()
-        a = lookup(plan.flags["a"], case).astype(F32)
-        big_a = 2.0 * lookup(plan.flags["big_a"], case).astype(F32)
+        a = flags_ref[3].astype(F32)
+        big_a = 2.0 * flags_ref[4].astype(F32)
         is_fine = places_ref[3]
         d = is_fine * a + (1.0 - is_fine) * big_a
         row = places_ref[1] + d + (lax.axis_index("lat") * rows).astype(F32)
@@ -458,50 +448,49 @@
         hot = jnp.where(lane == ids + wrapped, 1.0, 0.0).astype(BF16)
         fine_ref[...] = hot[: len(fine)]
         coarse_ref[...] = hot[len(fine) :]
-
-    outs = shapes([len(fine), len(coarse)], 128)
+        for copy in later:
+            copy.wait()
+
+    outs = shapes([len(fine), len(coarse)], 128) + [pltpu.VMEM(w.shape, BF16) for w in weights]
     scratch = [pltpu.VMEM(flat_regions.shape, I32), pltpu.VMEM(places.shape, F32)]
-    return call(
-        body, outs, [VMEM] * 2, shifts, [flat_regions, places], [HBM] * 2, scratch, 2, 1 << 28, 4 << 20
-    )
-
-
-def fine_level(shifts, tokens, pieces, key_id, w_qkv, w_proj, plan):
-    _, rows, cols, width = tokens.shape
-    count = 2 * rows * cols
+    args = [flags, flat_regions, places, *weights]
+    in_specs = [SMEM] + [HBM] * (2 + len(weights))
+    fine_id, coarse_id, *weights = call(body, outs, args, in_specs, scratch, 2 + len(weights), 1 << 28, 4 << 20)
+    return fine_id, coarse_id, weights
+
+
+def fetch(weights):
+    def body(*refs):
+        sems = refs[-1]
+        start = Copies(sems)
+        for copy in [start(src, dst) for src, dst in zip(refs[: len(weights)], refs[len(weights) : -1])]:
+            copy.wait()
+
+    outs = [pltpu.VMEM(w.shape, BF16) for w in weights]
+    size = sum(2 * w.size for w in weights)
+    return call(body, outs, weights, [HBM] * len(weights), [], len(weights), 0, size)
+
+
+def fine_level(flags, tokens, pieces, key_id, w_qkv, w_proj, rows, plan):
+    count, width = tokens.shape
     inner = w_proj.shape[0]
     kinds = 3 * len(plan.two)
 
-    def body(shifts_ref, tokens_hbm, *refs):
+    def body(flags_ref, tokens_ref, *refs):
         piece_refs, refs = refs[: len(pieces)], refs[len(pieces) :]
-        id_hbm, qkv_w_hbm, proj_w_hbm, table_ref, out_hbm, *refs = refs
-        piece_outs, refs = refs[:kinds], refs[kinds:]
-        tokens_ref, source_ref, id_ref, qkv_w_ref, proj_w_ref, rows_ref, x_ref, qkv_ref, out_ref, sems = refs
-        case = case_of(shifts_ref)
-        start = Copies(sems)
-        held = start(tokens_hbm, tokens_ref)
-        index = start(table_ref.at[case], rows_ref)
-        got = Pieces(piece_refs, plan.one, lookup(plan.flags["one_class"], case), source_ref, count, sems, 12)
-        qkv_w, proj_w, ids = start(qkv_w_hbm, qkv_w_ref), start(proj_w_hbm, proj_w_ref), start(id_hbm, id_ref)
-        index.wait()
+        id_ref, qkv_w_ref, proj_w_ref, rows_ref, out_ref, *refs = refs
+        piece_outs, (source_ref, x_ref, qkv_ref, _) = refs[:kinds], refs[kinds:]
+        lay_pieces(piece_refs, plan.one, flags_ref[0], source_ref)
         take = columns_of(rows_of(plan, rows_ref, "take_one"), count)
-        held.wait()
-        source_ref[:count, :] = flat(tokens_ref)
-        got.wait()
-        x = select_rows(take, source_ref[...])
+        x = select_rows(take, tokens_ref[...]) + select_rows(take - float(count), source_ref[...])
         x_ref[...] = x
         normed = layer_norm(x).astype(BF16)
-        qkv_w.wait()
         qkv_ref[...] = jnp.dot(normed, qkv_w_ref[...], preferred_element_type=F32).astype(BF16)
-        proj_w.wait()
-        ids.wait()
-        leave = []
 
         def finish(w, out):
             at = slice(w * TOK, (w + 1) * TOK)
             out = lax.dot_general(out, proj_w_ref[...], TN, preferred_element_type=F32)
             out_ref[at, :] = (x_ref[at, :] + out).astype(BF16)
-            leave.append(start(out_ref.at[pl.ds(w * TOK, TOK)], out_hbm.at[pl.ds(w * TOK, TOK)]))
 
         attend_windows(
             lambda w, at: qkv_ref[w * TOK : (w + 1) * TOK, at : at + 128],
@@ -510,79 +499,47 @@
             inner,
             finish,
         )
-        which = lookup(plan.flags["two_class"], case)
-        send_classes(plan, rows_ref, "send_two", out_ref, plan.two, which, piece_outs)
-        for copy in leave:
-            copy.wait()
-
-    outs = shapes([count], width, pltpu.HBM) + [shape for size in plan.two for shape in shapes(size, width)]
-    specs = [HBM] + [VMEM] * kinds
+        send_classes(plan, rows_of(plan, rows_ref, "send_two"), out_ref, plan.two, flags_ref[1], piece_outs)
+
+    outs = shapes([count], width) + [shape for size in plan.two for shape in shapes(size, width)]
     scratch = [
-        pltpu.VMEM(tokens.shape, BF16),
-        pltpu.VMEM((count + sum(plan.one[-1]), width), BF16),
-        pltpu.VMEM(key_id.shape, BF16),
-        pltpu.VMEM(w_qkv.shape, BF16),
-        pltpu.VMEM(w_proj.shape, BF16),
-        pltpu.VMEM(plan.table.shape[1:], F32),
+        pltpu.VMEM((sum(plan.one[-1]), width), BF16),
         pltpu.VMEM((count, width), F32),
         pltpu.VMEM((count, 3 * inner), BF16),
-        pltpu.VMEM((count, width), BF16),
     ]
-    args = [tokens, *pieces, key_id, w_qkv, w_proj, plan.table]
-    in_specs = [HBM] + [ANY] * (len(pieces) + 1) + [HBM] * 3
-    assert 5 + count // TOK <= 16
-    out, *sent = call(body, outs, specs, shifts, args, in_specs, scratch, 16, 3 << 30, 6 << 20)
+    args = [flags, tokens, *pieces, key_id, w_qkv, w_proj, rows]
+    out, *sent = call(body, outs, args, [SMEM] + [VMEM] * (len(args) - 1), scratch, 1, 3 << 30, 6 << 20)
     return out, sent
 
 
-def coarse_level(shifts, fine, pieces, key_id, w_merge, w_qkv, w_proj, plan):
+def coarse_level(flags, fine, pieces, key_id, w_merge, w_qkv, w_proj, rows, plan):
     count = key_id.shape[0]
     width = w_merge.shape[1]
     own, half = fine.shape
     inner = w_proj.shape[0]
     kinds = 3 * len(plan.three)
-    step = w_merge.shape[0] // 4
-
-    def body(shifts_ref, fine_hbm, *refs):
+
+    def body(flags_ref, fine_ref, *refs):
         piece_refs, refs = refs[: len(pieces)], refs[len(pieces) :]
-        id_hbm, merge_hbm, qkv_w_hbm, proj_w_hbm, table_ref, out_hbm, *refs = refs
-        piece_outs, refs = refs[:kinds], refs[kinds:]
-        source_ref, id_ref, merge_ref, qkv_w_ref, proj_w_ref, rows_ref, qkv_ref, out_ref, sems = refs
-        case = case_of(shifts_ref)
-        start = Copies(sems)
-        index = start(table_ref.at[case], rows_ref)
-        held = start(fine_hbm, source_ref.at[pl.ds(0, own)])
-        got = Pieces(piece_refs, plan.two, lookup(plan.flags["two_class"], case), source_ref, own, sems, 12)
-        merge_w = [
-            start(merge_hbm.at[pl.ds(n * step, step)], merge_ref.at[pl.ds(n * step, step)]) for n in range(4)
-        ]
-        qkv_w, proj_w, ids = start(qkv_w_hbm, qkv_w_ref), start(proj_w_hbm, proj_w_ref), start(id_hbm, id_ref)
-        index.wait()
+        id_ref, merge_ref, qkv_w_ref, proj_w_ref, rows_ref, out_ref, *refs = refs
+        piece_outs, (source_ref, qkv_ref, _) = refs[:kinds], refs[kinds:]
+        lay_pieces(piece_refs, plan.two, flags_ref[1], source_ref)
         take = columns_of(rows_of(plan, rows_ref, "take_two"), 4 * count)
-        held.wait()
-        got.wait()
-        x = select_rows(take, source_ref[...])
+        x = select_rows(take, fine_ref[...]) + select_rows(take - float(own), source_ref[...])
         x = jnp.concatenate([x[n * count : (n + 1) * count] for n in range(4)], axis=1)
         stacked = layer_norm(x).astype(BF16)
-        for copy in merge_w:
-            copy.wait()
         merged = jnp.dot(stacked, merge_ref[...], preferred_element_type=F32).astype(BF16).astype(F32)
         normed = layer_norm(merged).astype(BF16)
-        qkv_w.wait()
         qkv_ref[...] = jnp.dot(normed, qkv_w_ref[...], preferred_element_type=F32).astype(BF16)
-        ids.wait()
-        proj_w.wait()
 
         def finish(w, out):
             out = lax.dot_general(out, proj_w_ref[...], TN, preferred_element_type=F32)
             out_ref[...] = (merged + out).astype(BF16)
 
         attend_windows(lambda w, at: qkv_ref[:, at : at + 128], lambda w: id_ref[...], 1, inner, finish)
-        leave = start(out_ref, out_hbm)
-        which = lookup(plan.flags["three_class"], case)
         for n, (sizes, fine_sizes) in enumerate(zip(plan.three, plan.four)):
 
-            @pl.when(which == n)
+            @pl.when(flags_ref[2] == n)
             def _():
                 sent = select_rows(columns_of(rows_of(plan, rows_ref, "send_three"), sum(sizes)), out_ref[...])
                 sent = sent.astype(BF16)
@@ -593,124 +550,102 @@
                     at += size
                 if sum(fine_sizes):
                     index = columns_of(rows_of(plan, rows_ref, "send_four"), sum(fine_sizes))
-                    sent = select_rows(index, source_ref[:own, :]).astype(BF16)
+                    sent = select_rows(index, fine_ref[...]).astype(BF16)
                     at = 0
                     for ref, size, more in zip(piece_outs[3 * n :], sizes, fine_sizes):
                         ref[2 * size :, :] = sent[at : at + more]
                         at += more
 
-        leave.wait()
-
-    outs = shapes([count], width, pltpu.HBM)
+    outs = shapes([count], width)
     for sizes, fine_sizes in zip(plan.three, plan.four):
         outs += shapes([2 * n + m for n, m in zip(sizes, fine_sizes)], half)
-    specs = [HBM] + [VMEM] * kinds
-    scratch = [
-        pltpu.VMEM((own + sum(plan.two[-1]), half), BF16),
-        pltpu.VMEM(key_id.shape, BF16),
-        pltpu.VMEM(w_merge.shape, BF16),
-        pltpu.VMEM(w_qkv.shape, BF16),
-        pltpu.VMEM(w_proj.shape, BF16),
-        pltpu.VMEM(plan.table.shape[1:], F32),
-        pltpu.VMEM((count, 3 * inner), BF16),
-        pltpu.VMEM((count, width), BF16),
-    ]
-    args = [fine, *pieces, key_id, w_merge, w_qkv, w_proj, plan.table]
-    in_specs = [HBM] + [ANY] * (len(pieces) + 1) + [HBM] * 4
-    out, *sent = call(body, outs, specs, shifts, args, in_specs, scratch, 16, 3 << 30, 12 << 20)
+    scratch = [pltpu.VMEM((sum(plan.two[-1]), half), BF16), pltpu.VMEM((count, 3 * inner), BF16)]
+    args = [flags, fine, *pieces, key_id, w_merge, w_qkv, w_proj, rows]
+    out, *sent = call(body, outs, args, [SMEM] + [VMEM] * (len(args) - 1), scratch, 1, 3 << 30, 12 << 20)
     return out, sent
 
 
-def fine_output(shifts, fine, pieces, got, which, plan, rows, cols):
+def fine_output(flags, fine, pieces, rows, plan, block_rows, block_cols, partial):
     own, width = fine.shape
-    room = sum(plan.two[-1])
-    extra = plan.four[which]
-
-    def body(shifts_ref, fine_hbm, *refs):
-        piece_refs, refs = refs[: len(pieces)], refs[len(pieces) :]
-        got_refs, refs = refs[: len(got)], refs[len(got) :]
-        table_ref, out_ref, source_ref, rows_ref, sems = refs
-        case = case_of(shifts_ref)
-        start = Copies(sems)
-        waits = [start(table_ref.at[case], rows_ref), start(fine_hbm, source_ref.at[pl.ds(0, own)])]
-        at = own + room
-        for ref, size, more in zip(got_refs, plan.three[which], extra):
-            waits.append(start(ref.at[pl.ds(2 * size, more)], source_ref.at[pl.ds(at, more)]))
-            at += more
-        pieces_in = Pieces(piece_refs, plan.two, lookup(plan.flags["two_class"], case), source_ref, own, sems, 8)
-        for copy in waits:
-            copy.wait()
+
+    def body(flags_ref, fine_ref, *refs):
+        piece_refs, (rows_ref, out_ref, source_ref, _) = refs[: len(pieces)], refs[len(pieces) :]
+        lay_pieces(piece_refs, plan.two, flags_ref[1], source_ref)
         take = columns_of(rows_of(plan, rows_ref, "fine_out"), own)
-        pieces_in.wait()
-        out = select_rows(take, source_ref[...])
-        out_ref[...] = out.reshape(2, rows, cols, width).astype(BF16)
-
-    outs = [jax.ShapeDtypeStruct((2, rows, cols, width), BF16)]
-    scratch = [
-        pltpu.VMEM((own + room + (sum(extra) if got else 0), width), BF16),
-        pltpu.VMEM(plan.table.shape[1:], F32),
-    ]
-    args = [fine, *pieces, *got, plan.table]
-    in_specs = [HBM] + [ANY] * (len(pieces) + len(got)) + [HBM]
-    return call(body, outs, [VMEM], shifts, args, in_specs, scratch, 16, 1 << 30, 4 << 20)[0]
-
-
-def coarse_output(shifts, coarse, got, which, plan, rows, cols):
+        out = select_rows(take, fine_ref[...]) + select_rows(take - float(own), source_ref[...])
+        out_ref[...] = (out if partial else out.reshape(out_ref.shape)).astype(BF16)
+
+    outs = [jax.ShapeDtypeStruct((2, block_rows, block_cols, width), BF16)]
+    if partial:
+        outs = shapes([own], width)
+    scratch = [pltpu.VMEM((sum(plan.two[-1]), width), BF16)]
+    args = [flags, fine, *pieces, rows]
+    return call(body, outs, args, [SMEM] + [VMEM] * (len(args) - 1), scratch, 1, 1 << 30, 4 << 20)[0]
+
+
+def coarse_output(coarse, got, rows, which, plan, block_rows, block_cols, part=None):
     own, width = coarse.shape
     half = width // 2
-    sizes = plan.three[which]
-
-    def body(shifts_ref, coarse_hbm, *refs):
-        got_refs, (table_ref, out_ref, source_ref, rows_ref, sems) = refs[:3], refs[3:]
-        start = Copies(sems)
-        waits = [start(table_ref.at[case_of(shifts_ref)], rows_ref), start(coarse_hbm, source_ref.at[pl.ds(0, own)])]
-        at = own
-        for ref, size in zip(got_refs, sizes):
-            for n in range(2):
-                to = source_ref.at[pl.ds(at, size), pl.ds(n * half, half)]
-                waits.append(start(ref.at[pl.ds(n * size, size)], to))
-            at += size
-        for copy in waits:
-            copy.wait()
+    sizes, more = plan.three[which], plan.four[which]
+    parts = [] if part is None else [part]
+
+    def body(coarse_ref, *refs):
+        got_refs, refs = refs[:3], refs[3:]
+        part_refs, (rows_ref, out_ref, *fine_outs, _) = refs[: len(parts)], refs[len(parts) :]
+        back = [
+            jnp.concatenate([ref[:size, :], ref[size : 2 * size, :]], axis=1) for ref, size in zip(got_refs, sizes)
+        ]
         take = columns_of(rows_of(plan, rows_ref, "coarse_out"), own)
-        out = select_rows(take, source_ref[...]).astype(BF16)
+        out = select_rows(take, stack_rows([coarse_ref[...]] + back)).astype(BF16)
         for n in range(own // 2):
-            out_ref[n // cols, n % cols] = out[2 * n : 2 * n + 2]
-
-    outs = [jax.ShapeDtypeStruct((rows, cols, 2, width), BF16)]
-    scratch = [pltpu.VMEM((own + sum(sizes), width), BF16), pltpu.VMEM(plan.table.shape[1:], F32)]
-    args = [coarse, *got, plan.table]
-    out = call(body, outs, [VMEM], shifts, args, [HBM] + [ANY] * 3 + [HBM], scratch, 8, 1 << 28, 1 << 20)[0]
-    return out.transpose(2, 0, 1, 3)
+            out_ref[n // block_cols, n % block_cols] = out[2 * n : 2 * n + 2]
+        for part_ref, fine_ref in zip(part_refs, fine_outs):
+            fine = stack_rows([ref[2 * size :, :] for ref, size in zip(got_refs, sizes)])
+            base = part_ref.shape[0] + sum(plan.two[-1])
+            take = columns_of(rows_of(plan, rows_ref, "fine_out"), part_ref.shape[0]) - float(base)
+            out = part_ref[...].astype(F32) + select_rows(take, fine)
+            fine_ref[...] = out.reshape(fine_ref.shape).astype(BF16)
+
+    outs = [jax.ShapeDtypeStruct((block_rows, block_cols, 2, width), BF16)]
+    outs += [jax.ShapeDtypeStruct((2, 2 * block_rows, 2 * block_cols, half), BF16) for _ in parts]
+    args = [coarse, *got, *parts, rows]
+    out, *fine = call(body, outs, args, [VMEM] * len(args), [], 1, 1 << 28, 1 << 20)
+    return out.transpose(2, 0, 1, 3), *fine
 
 
 def on_device(tokens, regions, shifts, fine_qkv, fine_proj, merge_weight, coarse_qkv, coarse_proj):
     _, rows, cols, _ = tokens.shape
     plan = Plan(rows, cols)
 
-    def first(which, sign, sent, shifts, regions):
+    def first(which, sign, sent, flags, regions, weights):
         got = exchange_class(sent, which, sign)
-        return got, id_kernel(shifts, regions, plan, rows, cols)
-
-    def second(which, sign, sent):
-        return exchange_class(sent, which, sign)
-
-    def third(which, sign, sent, shifts, fine, pieces, coarse):
+        return got, id_kernel(flags, regions, weights, plan, rows, cols)
+
+    def second(which, sign, sent, weights):
+        return exchange_class(sent, which, sign), fetch(weights)
+
+    def third(which, sign, sent, flags, fine, pieces, coarse, table):
         got = exchange(sent[3 * which : 3 * which + 3], sign)
-        fine_out = fine_output(shifts, fine, pieces, got if which else [], which, plan, rows, cols)
-        return fine_out, coarse_output(shifts, coarse, got, which, plan, rows // 2, cols // 2)
+        fine_out = fine_output(flags, fine, pieces, table, plan, rows, cols, which == 1)
+        place = (table, which, plan, rows // 2, cols // 2)
+        if which == 1:
+            coarse_out, fine_out = coarse_output(coarse, got, *place, part=fine_out)
+        else:
+            (coarse_out,) = coarse_output(coarse, got, *place)
+        return fine_out, coarse_out
 
     def branches(stage, pairs):
         return [functools.partial(stage, which, sign) for which, sign in pairs]
 
-    sent, one, two, three = first_pieces(shifts, tokens, plan)
-    got, (fine_id, coarse_id) = choose(one, branches(first, plan.one_branches), sent, shifts, regions)
-    fine, sent = fine_level(shifts, tokens, got, fine_id, fine_qkv, fine_proj, plan)
-    got = choose(two, branches(second, plan.two_branches), sent)
-    coarse, sent = coarse_level(
-        shifts, fine, got, coarse_id, merge_weight, coarse_qkv, coarse_proj, plan
+    sent, source, table, flags, one, two, three = first_pieces(shifts, tokens, plan)
+    got, (fine_id, coarse_id, weights) = choose(
+        one, branches(first, plan.one_branches), sent, flags, regions, [fine_qkv, fine_proj]
     )
-    return choose(three, branches(third, plan.three_branches), sent, shifts, fine, got, coarse)
+    fine, sent = fine_level(flags, source, got, fine_id, *weights, table, plan)
+    weights = [merge_weight, coarse_qkv, coarse_proj]
+    got, weights = choose(two, branches(second, plan.two_branches), sent, weights)
+    coarse, sent = coarse_level(flags, fine, got, coarse_id, *weights, table, plan)
+    return choose(three, branches(third, plan.three_branches), sent, flags, fine, got, coarse, table)
 
 
 def solution(mesh):

time: 52.6 us -> 57.3 us (1.089)
  local copies, waits for them, and re-layouts: 0.01 us -> 11.5 us
  waiting for transfers between devices: 8.25 us -> 3.9 us
  starting transfers between devices: 14.2 us -> 12.2 us
  Pallas kernels: 26.6 us -> 25.9 us
    unnamed x2 -> x12, local copies, waits for them, and re-layouts: 0.01 us -> 7.81 us
    ppermute x3, starting transfers between devices: 8.09 us -> 3.98 us  [exchange(): both = lax.ppermute(both, ('lat', 'lon'), pairs)]
    ppermute x3, waiting for transfers between devices: 7.86 us -> 3.88 us  [exchange(): both = lax.ppermute(both, ('lat', 'lon'), pairs)]
    cond x0 -> x4, local copies, waits for them, and re-layouts: none -> 3.72 us
    ppermute x3, starting transfers between devices: 5.01 us -> 6.61 us  [exchange(): col = lax.ppermute(col, 'lon', [((j + sign) % lon, j) for j in range(lon)])]
    pallas_call x9 -> x10, Pallas kernels: 26.6 us -> 25.9 us  [the longest x7 24.4 us: call(): pl.pallas_call(body, out_shape=outs, in_specs=in_specs, out_specs=out_spe...]
  transfers between devices with their start and end apart: 9 -> 9, of which waited for: 4 -> 1; matrix products, arithmetic and copies ran while one was open for 0% -> 0% of each run, Pallas kernels for 11% -> 17%
where the time goes in v1:
time: 57.3 us; the launch traced here: 56.6 us
  Pallas kernels  25.9 us (45%)
  starting transfers between devices  12.2 us (21%)
  local copies, waits for them, and re-layouts  11.5 us (20%)
  waiting for transfers between devices  3.9 us (7%)
  loops' own time  2.17 us (4%)
  between operations  0.86 us (2%)
    pallas_call x7, Pallas kernels, call(): pl.pallas_call(body, out_shape=outs, in_specs=in_specs, out_specs=out_spe...  24.4 us
    unnamed x12, local copies, waits for them, and re-layouts  7.81 us
    ppermute x3, starting transfers between devices, exchange(): col = lax.ppermute(col, 'lon', [((j + sign) % lon, j) for j in range(lon)])  6.61 us
    ppermute x3, starting transfers between devices, exchange(): both = lax.ppermute(both, ('lat', 'lon'), pairs)  3.98 us
    ppermute x3, waiting for transfers between devices, exchange(): both = lax.ppermute(both, ('lat', 'lon'), pairs)  3.88 us
    cond x4, local copies, waits for them, and re-layouts  3.72 us
    another operation x3, loops' own time, choose(): lax.cond_p.bind(index, *flat_args, branches=tuple((closed(branch) for bra...  2.17 us
    ppermute x3, starting transfers between devices, exchange(): row = lax.ppermute(row, 'lat', [((i + sign) % lat, i) for i in range(lat)])  1.64 us
  transfers between devices with their start and end apart: 9, of which 1 were waited for; matrix products, arithmetic and copies ran while one was open for 0% of the time, Pallas kernels for 17%

profile of v1, /device:TPU:0, one launch (start us, length us, event | category | flops | bytes accessed | tf_op | source)
XLA Modules:
  0.0 56.6 jit_solution(7572499970443329215)
XLA Ops:
  0.6 2.1 %shard_map.110 = (bf16[48,512]{1,0:T(8,128)(2,1)S(1)}, bf16[48,512]{1,0:T(8,128)(2,1)S(1)}, bf16[16,512]{1,0:T(8,128)(2,1)S(1)}, bf16[112,512]{1,0:T(8,128)(2,1)...) custom-call(s32[2]{0:T(128)} %shifts_hbm.1, ...), custom_call_target="tpu_custom_call" | custom-call | flops 268435456 | bytes 1048576 | tf_op jit(solution)/shard_map/pallas_call | solution.py:264
  2.7 0.0 copy-start.12
  2.8 0.8 %copy-done.12 = bf16[576,512]{1,0:T(8,128)(2,1)} copy-done((bf16[576,512]{1,0:T(8,128)(2,1)}, bf16[576,512]{1,0:T(8,128)(2,1)S(1)}, u32[]{:S(2)}) %copy-start.12) | copy-done | bytes 589848
  3.6 12.4 %conditional.3 = (bf16[48,512]{1,0:T(8,128)(2,1)}, bf16[48,512]{1,0:T(8,128)(2,1)}, bf16[16,512]{1,0:T(8,128)(2,1)}, bf16[112,512]{1,0:T(8,128)(2,1)}, bf16[112,...) conditional(s32[]{:T(128)} %bitcast.8, ...), branch_computations={%region_0.0_spmd, %region_1.0_spmd, %region_2.0_spmd, %region_3.0_... | conditional | flops 268435456 | bytes 5308616 | solution.py:357
  4.2 0.5 collective-permute-start.6
  4.7 2.6 %collective-permute-start.7 = (bf16[112,512]{1,0:T(8,128)(2,1)S(1)}, bf16[112,512]{1,0:T(8,128)(2,1)}, u32[]{:S(2)}, u32[]{:S(2)}) collective-permute-start(bf16[112,512]{1,0:T(8,128)(2,1)S(1)} %get-tuple-element.244), channel_id=1, source_target_pairs={{3,0},{0,1},{1,2},{2,3},{7,4},{4,5},{5,6},{6,7},{11,8},{8,9},{9,10... | collective-permute-start | bytes 344072 | tf_op jit(solution)/shard_map/cond/branch_2_fun/ppermute | solution.py:332
  7.4 2.4 %collective-permute-start.8 = (bf16[48,512]{1,0:T(8,128)(2,1)S(1)}, bf16[48,512]{1,0:T(8,128)(2,1)}, u32[]{:S(2)}, u32[]{:S(2)}) collective-permute-start(bf16[48,512]{1,0:T(8,128)(2,1)S(1)} %get-tuple-element.245), channel_id=1, source_target_pairs={{31,0},{28,1},{29,2},{30,3},{3,4},{0,5},{1,6},{2,7},{7,8},{4,9},{5... | collective-permute-start | bytes 147464 | tf_op jit(solution)/shard_map/cond/branch_2_fun/ppermute | solution.py:333
  9.8 0.7 %branch_2_fun.7 = (bf16[48,512]{1,0:T(8,128)(2,1)}, bf16[48,512]{1,0:T(8,128)(2,1)}, bf16[16,512]{1,0:T(8,128)(2,1)}) custom-call(), custom_call_target="tpu_custom_call" | custom-call | tf_op jit(solution)/shard_map/cond/branch_2_fun/pallas_call | solution.py:340
  10.5 1.6 %branch_2_fun.8 = (bf16[576,128]{1,0:T(8,128)(2,1)S(1)}, bf16[144,128]{1,0:T(8,128)(2,1)S(1)}, bf16[512,1536]{1,0:T(8,128)(2,1)S(1)}, bf16[512,512]{1,0:T(8,128)(2,1)S(1)}) custom-call(s32[8]{0:T(128)S(4)} %get-tuple-element.246.flags_ref, s32[192,96]{1,0:T(8,128)} %bitcast.12, f32[4,6,128]{2,1,0:T(8,128)} %constant.5.clone.places_hbm, ...), custom_call_target="tpu_custom_call" | custom-call | flops 268435456 | bytes 4194304 | tf_op jit(solution)/shard_map/cond/branch_2_fun/pallas_call | solution.py:264
  12.1 3.9 %collective-permute-done.8 = bf16[48,512]{1,0:T(8,128)(2,1)} collective-permute-done((bf16[48,512]{1,0:T(8,128)(2,1)S(1)}, bf16[48,512]{1,0:T(8,128)(2,1)}, u32[]{:S(2)}, u32[]{:S(2)}) %collective-permute-start.8) | collective-permute-done | bytes 49184 | tf_op jit(solution)/shard_map/cond/branch_2_fun/ppermute | solution.py:333
  16.0 0.0 collective-permute-done.6
  16.0 0.0 collective-permute-done.7
  16.0 0.0 copy-start.13
  16.0 1.1 %copy-done.13 = bf16[576,512]{1,0:T(8,128)(2,1)S(1)} copy-done((bf16[576,512]{1,0:T(8,128)(2,1)S(1)}, bf16[576,512]{1,0:T(8,128)(2,1)}, u32[]{:S(2)}) %copy-start.13) | copy-done | bytes 589848
  17.0 7.6 %shard_map.111 = (bf16[576,512]{1,0:T(8,128)(2,1)S(1)}, bf16[48,512]{1,0:T(8,128)(2,1)S(1)}, bf16[48,512]{1,0:T(8,128)(2,1)S(1)}, bf16[16,512]{1,0:T(8,128)(2,1)...) custom-call(s32[8]{0:T(128)S(4)} %get-tuple-element.447.flags_ref, ...), custom_call_target="tpu_custom_call" | custom-call | flops 3221225472 | bytes 6291456 | tf_op jit(solution)/shard_map/pallas_call | solution.py:264
  24.6 0.0 copy-start.14
  24.6 0.8 %copy-done.14 = bf16[576,512]{1,0:T(8,128)(2,1)} copy-done((bf16[576,512]{1,0:T(8,128)(2,1)}, bf16[576,512]{1,0:T(8,128)(2,1)S(1)}, u32[]{:S(2)}) %copy-start.14) | copy-done | bytes 589848
  25.5 11.4 %conditional.4 = (bf16[48,512]{1,0:T(8,128)(2,1)S(1)}, bf16[48,512]{1,0:T(8,128)(2,1)S(1)}, bf16[16,512]{1,0:T(8,128)(2,1)S(1)}, bf16[128,512]{1,0:T(8,128)(2,1)...) conditional(s32[]{:T(128)} %bitcast.9, ...), branch_computations={%region_4.0_spmd, %region_5.0_spmd, %region_6.0_spmd, %region_7.0_... | conditional | bytes 39518480 | solution.py:357
  26.2 0.6 %collective-permute-start.18 = (bf16[128,512]{1,0:T(8,128)(2,1)S(1)}, bf16[128,512]{1,0:T(8,128)(2,1)}, u32[]{:S(2)}, u32[]{:S(2)}) collective-permute-start(bf16[128,512]{1,0:T(8,128)(2,1)S(1)} %get-tuple-element.301), channel_id=1, source_target_pairs={{4,0},{8,4},{12,8},{16,12},{20,16},{24,20},{28,24},{0,28},{5,1},{9... | collective-permute-start | bytes 393224 | tf_op jit(solution)/shard_map/cond/branch_2_fun/ppermute | solution.py:334
  26.8 1.7 %collective-permute-start.19 = (bf16[128,512]{1,0:T(8,128)(2,1)S(1)}, bf16[128,512]{1,0:T(8,128)(2,1)}, u32[]{:S(2)}, u32[]{:S(2)}) collective-permute-start(bf16[128,512]{1,0:T(8,128)(2,1)S(1)} %get-tuple-element.302), channel_id=1, source_target_pairs={{1,0},{2,1},{3,2},{0,3},{5,4},{6,5},{7,6},{4,7},{9,8},{10,9},{11,1... | collective-permute-start | bytes 393224 | tf_op jit(solution)/shard_map/cond/branch_2_fun/ppermute | solution.py:332
  28.5 0.4 collective-permute-start.20
  28.9 0.8 %branch_2_fun.10 = (bf16[160,512]{1,0:T(8,128)(2,1)}, bf16[160,512]{1,0:T(8,128)(2,1)}, bf16[112,512]{1,0:T(8,128)(2,1)}) custom-call(), custom_call_target="tpu_custom_call" | custom-call | tf_op jit(solution)/shard_map/cond/branch_2_fun/pallas_call | solution.py:340
  29.7 3.4 %branch_2_fun.11 = (bf16[2048,1024]{1,0:T(8,128)(2,1)S(1)}, bf16[1024,1536]{1,0:T(8,128)(2,1)S(1)}, bf16[512,1024]{1,0:T(8,128)(2,1)S(1)}) custom-call(bf16[2048,1024]{1,0:T(8,128)(2,1)} %get-tuple-element.307.refs_0_, bf16[1024,1536]{1,0:T(8,128)(2,1)} %get-tuple-element.308.refs_1_, bf16[512,1024]{1,0:T(8,128)(2,1)} %get-tuple-element.309.refs_2_), custom_call_target="tpu_custom_call" | custom-call | bytes 8388608 | tf_op jit(solution)/shard_map/cond/branch_2_fun/pallas_call | solution.py:264
  33.1 0.0 copy-start.2
  33.1 2.0 %copy-done.2 = bf16[2048,1024]{1,0:T(8,128)(2,1)} copy-done((bf16[2048,1024]{1,0:T(8,128)(2,1)}, bf16[2048,1024]{1,0:T(8,128)(2,1)S(1)}, u32[]{:S(2)}) %copy-start.2) | copy-done | bytes 4194328 | tf_op jit(solution)/shard_map/cond
  35.2 0.0 copy-start.8
  35.2 1.7 %copy-done.8 = bf16[1024,1536]{1,0:T(8,128)(2,1)} copy-done((bf16[1024,1536]{1,0:T(8,128)(2,1)}, bf16[1024,1536]{1,0:T(8,128)(2,1)S(1)}, u32[]{:S(2)}) %copy-start.8) | copy-done | bytes 3145752 | tf_op jit(solution)/shard_map/cond
  36.9 0.0 collective-permute-done.20
  36.9 0.0 collective-permute-done.18
  36.9 0.0 collective-permute-done.19
  36.9 0.0 copy-start.5
  36.9 2.2 %copy-done.5 = bf16[2048,1024]{1,0:T(8,128)(2,1)S(1)} copy-done((bf16[2048,1024]{1,0:T(8,128)(2,1)S(1)}, bf16[2048,1024]{1,0:T(8,128)(2,1)}, u32[]{:S(2)}) %copy-start.5) | copy-done | bytes 4194328
  39.1 0.0 copy-start.11
  39.1 1.9 %copy-done.11 = bf16[1024,1536]{1,0:T(8,128)(2,1)S(1)} copy-done((bf16[1024,1536]{1,0:T(8,128)(2,1)S(1)}, bf16[1024,1536]{1,0:T(8,128)(2,1)}, u32[]{:S(2)}) %copy-start.11) | copy-done | bytes 3145752
  41.0 0.0 copy-start.15
  41.0 1.1 %copy-done.15 = bf16[576,512]{1,0:T(8,128)(2,1)S(1)} copy-done((bf16[576,512]{1,0:T(8,128)(2,1)S(1)}, bf16[576,512]{1,0:T(8,128)(2,1)}, u32[]{:S(2)}) %copy-start.15) | copy-done | bytes 589848
  42.0 5.6 %shard_map.112 = (bf16[144,1024]{1,0:T(8,128)(2,1)S(1)}, bf16[64,512]{1,0:T(8,128)(2,1)S(1)}, bf16[64,512]{1,0:T(8,128)(2,1)S(1)}, bf16[32,512]{1,0:T(8,128)(2,1...) custom-call(s32[8]{0:T(128)S(4)} %get-tuple-element.447.flags_ref, ...), custom_call_target="tpu_custom_call" | custom-call | flops 3221225472 | bytes 12582912 | tf_op jit(solution)/shard_map/pallas_call | solution.py:264
  47.7 8.7 %conditional.5 = (bf16[2,12,24,512]{3,2,1,0:T(8,128)(2,1)}, bf16[2,6,12,1024]{3,0,2,1:T(2,128)(2,1)}) conditional(s32[]{:T(128)} %bitcast.7, (s32[8]{0:T(128)S(4)}, bf16[576,512]{1,0:T(8,128)(2,1)S(1)}, bf16[48,512]{1,0:T(8,128)(2,1)S(1)}, bf16[48,512]{1,0:T(8,128)(2,1)S(1)}, bf16[16,512]{1,0:T(8,128)(2,1)S(1)}, ...), branch_computations={%region_9.0_spmd, %region_10.0_spmd, %region_11.0_spmd} | conditional | flops 1342177280 | bytes 6881416 | solution.py:357
  48.4 1.2 %collective-permute-start.32 = (bf16[32,512]{1,0:T(8,128)(2,1)S(1)}, bf16[32,512]{1,0:T(8,128)(2,1)S(1)}, u32[]{:S(2)}, u32[]{:S(2)}) collective-permute-start(bf16[32,512]{1,0:T(8,128)(2,1)S(1)} %get-tuple-element.374), channel_id=1, source_target_pairs={{5,0},{6,1},{7,2},{4,3},{9,4},{10,5},{11,6},{8,7},{13,8},{14,9},{1... | collective-permute-start | bytes 98312 | tf_op jit(solution)/shard_map/cond/branch_1_fun/ppermute | solution.py:333
  49.6 0.5 collective-permute-start.30
  50.1 2.2 %collective-permute-start.31 = (bf16[64,512]{1,0:T(8,128)(2,1)S(1)}, bf16[64,512]{1,0:T(8,128)(2,1)S(1)}, u32[]{:S(2)}, u32[]{:S(2)}) collective-permute-start(bf16[64,512]{1,0:T(8,128)(2,1)S(1)} %get-tuple-element.373), channel_id=1, source_target_pairs={{1,0},{2,1},{3,2},{0,3},{5,4},{6,5},{7,6},{4,7},{9,8},{10,9},{11,1... | collective-permute-start | bytes 196616 | tf_op jit(solution)/shard_map/cond/branch_1_fun/ppermute | solution.py:332
  52.3 3.0 %branch_1_fun.12 = bf16[2,12,24,512]{3,2,1,0:T(8,128)(2,1)} custom-call(s32[8]{0:T(128)S(4)} %get-tuple-element.359.flags_ref, bf16[576,512]{1,0:T(8,128)(2,1)S(1)} %get-tuple-element.360.fine_ref, bf16[48,512]{1,0:T(8,128)(2,1)S(1)} %get-tuple-element.361.refs_0_, bf16[48,512]{1,0:T(8,128)(2,1)S(1)} %get-tuple-element.362.refs_1_, ...), custom_call_target="tpu_custom_call" | custom-call | flops 1073741824 | bytes 4194304 | tf_op jit(solution)/shard_map/cond/branch_1_fun/pallas_call | solution.py:264
  55.3 0.0 collective-permute-done.32.refs_2_
  55.4 0.0 collective-permute-done.30.refs_0_
  55.4 0.0 collective-permute-done.31.refs_1_
  55.4 1.0 %branch_1_fun.13 = bf16[6,12,2,1024]{3,2,1,0:T(2,128)(2,1)} custom-call(bf16[144,1024]{1,0:T(8,128)(2,1)S(1)} %get-tuple-element.371.coarse_ref, bf16[64,512]{1,0:T(8,128)(2,1)S(1)} %collective-permute-done.30.refs_0_, bf16[64,512]{1,0:T(8,128)(2,1)S(1)} %collective-permute-done.31.refs_1_, bf16[32,512]{1,0:T(8,128)(2,1)S(1)} %collective-permute-done.32.refs_2_, ...), custom_call_target="tpu_custom_call" | custom-call | flops 268435456 | bytes 1048576 | tf_op jit(solution)/shard_map/cond/branch_1_fun/pallas_call | solution.py:264
  (1 shorter events, 0.0 us)
Async XLA Ops:
  2.7 0.8 %copy-start.12 = (bf16[576,512]{1,0:T(8,128)(2,1)}, bf16[576,512]{1,0:T(8,128)(2,1)S(1)}, u32[]{:S(2)}) copy-start(bf16[576,512]{1,0:T(8,128)(2,1)S(1)} %get-tuple-element.448.tokens_ref) | copy-start | bytes 1769476
  4.2 11.8 %collective-permute-start.6 = (bf16[112,512]{1,0:T(8,128)(2,1)S(1)}, bf16[112,512]{1,0:T(8,128)(2,1)}, u32[]{:S(2)}, u32[]{:S(2)}) collective-permute-start(bf16[112,512]{1,0:T(8,128)(2,1)S(1)} %get-tuple-element.243), channel_id=1, source_target_pairs={{28,0},{0,4},{4,8},{8,12},{12,16},{16,20},{20,24},{24,28},{29,1},{... | collective-permute-start | bytes 344072 | tf_op jit(solution)/shard_map/cond/branch_2_fun/ppermute | solution.py:334
  4.7 11.2 %collective-permute-start.7 = (bf16[112,512]{1,0:T(8,128)(2,1)S(1)}, bf16[112,512]{1,0:T(8,128)(2,1)}, u32[]{:S(2)}, u32[]{:S(2)}) collective-permute-start(bf16[112,512]{1,0:T(8,128)(2,1)S(1)} %get-tuple-element.244), channel_id=1, source_target_pairs={{3,0},{0,1},{1,2},{2,3},{7,4},{4,5},{5,6},{6,7},{11,8},{8,9},{9,10... | collective-permute-start | bytes 344072 | tf_op jit(solution)/shard_map/cond/branch_2_fun/ppermute | solution.py:332
  7.4 8.6 %collective-permute-start.8 = (bf16[48,512]{1,0:T(8,128)(2,1)S(1)}, bf16[48,512]{1,0:T(8,128)(2,1)}, u32[]{:S(2)}, u32[]{:S(2)}) collective-permute-start(bf16[48,512]{1,0:T(8,128)(2,1)S(1)} %get-tuple-element.245), channel_id=1, source_target_pairs={{31,0},{28,1},{29,2},{30,3},{3,4},{0,5},{1,6},{2,7},{7,8},{4,9},{5... | collective-permute-start | bytes 147464 | tf_op jit(solution)/shard_map/cond/branch_2_fun/ppermute | solution.py:333
  16.0 1.1 %copy-start.13 = (bf16[576,512]{1,0:T(8,128)(2,1)S(1)}, bf16[576,512]{1,0:T(8,128)(2,1)}, u32[]{:S(2)}) copy-start(bf16[576,512]{1,0:T(8,128)(2,1)} %copy-done.12) | copy-start | bytes 1769476
  24.6 0.8 %copy-start.14 = (bf16[576,512]{1,0:T(8,128)(2,1)}, bf16[576,512]{1,0:T(8,128)(2,1)S(1)}, u32[]{:S(2)}) copy-start(bf16[576,512]{1,0:T(8,128)(2,1)S(1)} %get-tuple-element.466.fine_ref) | copy-start | bytes 1769476
  26.2 10.7 %collective-permute-start.18 = (bf16[128,512]{1,0:T(8,128)(2,1)S(1)}, bf16[128,512]{1,0:T(8,128)(2,1)}, u32[]{:S(2)}, u32[]{:S(2)}) collective-permute-start(bf16[128,512]{1,0:T(8,128)(2,1)S(1)} %get-tuple-element.301), channel_id=1, source_target_pairs={{4,0},{8,4},{12,8},{16,12},{20,16},{24,20},{28,24},{0,28},{5,1},{9... | collective-permute-start | bytes 393224 | tf_op jit(solution)/shard_map/cond/branch_2_fun/ppermute | solution.py:334
  26.8 10.1 %collective-permute-start.19 = (bf16[128,512]{1,0:T(8,128)(2,1)S(1)}, bf16[128,512]{1,0:T(8,128)(2,1)}, u32[]{:S(2)}, u32[]{:S(2)}) collective-permute-start(bf16[128,512]{1,0:T(8,128)(2,1)S(1)} %get-tuple-element.302), channel_id=1, source_target_pairs={{1,0},{2,1},{3,2},{0,3},{5,4},{6,5},{7,6},{4,7},{9,8},{10,9},{11,1... | collective-permute-start | bytes 393224 | tf_op jit(solution)/shard_map/cond/branch_2_fun/ppermute | solution.py:332
  28.5 8.3 %collective-permute-start.20 = (bf16[48,512]{1,0:T(8,128)(2,1)S(1)}, bf16[48,512]{1,0:T(8,128)(2,1)}, u32[]{:S(2)}, u32[]{:S(2)}) collective-permute-start(bf16[48,512]{1,0:T(8,128)(2,1)S(1)} %get-tuple-element.303), channel_id=1, source_target_pairs={{5,0},{6,1},{7,2},{4,3},{9,4},{10,5},{11,6},{8,7},{13,8},{14,9},{1... | collective-permute-start | bytes 147464 | tf_op jit(solution)/shard_map/cond/branch_2_fun/ppermute | solution.py:333
  33.1 2.0 %copy-start.2 = (bf16[2048,1024]{1,0:T(8,128)(2,1)}, bf16[2048,1024]{1,0:T(8,128)(2,1)S(1)}, u32[]{:S(2)}) copy-start(bf16[2048,1024]{1,0:T(8,128)(2,1)S(1)} %get-tuple-element.572) | copy-start | bytes 12582916 | tf_op jit(solution)/shard_map/cond
  35.2 1.7 %copy-start.8 = (bf16[1024,1536]{1,0:T(8,128)(2,1)}, bf16[1024,1536]{1,0:T(8,128)(2,1)S(1)}, u32[]{:S(2)}) copy-start(bf16[1024,1536]{1,0:T(8,128)(2,1)S(1)} %get-tuple-element.573) | copy-start | bytes 9437188 | tf_op jit(solution)/shard_map/cond
  36.9 2.2 %copy-start.5 = (bf16[2048,1024]{1,0:T(8,128)(2,1)S(1)}, bf16[2048,1024]{1,0:T(8,128)(2,1)}, u32[]{:S(2)}) copy-start(bf16[2048,1024]{1,0:T(8,128)(2,1)} %get-tuple-element.487.refs_10_) | copy-start | bytes 12582916
  39.1 1.9 %copy-start.11 = (bf16[1024,1536]{1,0:T(8,128)(2,1)S(1)}, bf16[1024,1536]{1,0:T(8,128)(2,1)}, u32[]{:S(2)}) copy-start(bf16[1024,1536]{1,0:T(8,128)(2,1)} %get-tuple-element.488.refs_11_) | copy-start | bytes 9437188
  41.0 1.1 %copy-start.15 = (bf16[576,512]{1,0:T(8,128)(2,1)S(1)}, bf16[576,512]{1,0:T(8,128)(2,1)}, u32[]{:S(2)}) copy-start(bf16[576,512]{1,0:T(8,128)(2,1)} %copy-done.14) | copy-start | bytes 1769476
  48.4 7.0 %collective-permute-start.32 = (bf16[32,512]{1,0:T(8,128)(2,1)S(1)}, bf16[32,512]{1,0:T(8,128)(2,1)S(1)}, u32[]{:S(2)}, u32[]{:S(2)}) collective-permute-start(bf16[32,512]{1,0:T(8,128)(2,1)S(1)} %get-tuple-element.374), channel_id=1, source_target_pairs={{5,0},{6,1},{7,2},{4,3},{9,4},{10,5},{11,6},{8,7},{13,8},{14,9},{1... | collective-permute-start | bytes 98312 | tf_op jit(solution)/shard_map/cond/branch_1_fun/ppermute | solution.py:333
  49.6 5.8 %collective-permute-start.30 = (bf16[64,512]{1,0:T(8,128)(2,1)S(1)}, bf16[64,512]{1,0:T(8,128)(2,1)S(1)}, u32[]{:S(2)}, u32[]{:S(2)}) collective-permute-start(bf16[64,512]{1,0:T(8,128)(2,1)S(1)} %get-tuple-element.372), channel_id=1, source_target_pairs={{4,0},{8,4},{12,8},{16,12},{20,16},{24,20},{28,24},{0,28},{5,1},{9... | collective-permute-start | bytes 196616 | tf_op jit(solution)/shard_map/cond/branch_1_fun/ppermute | solution.py:334
  50.1 5.3 %collective-permute-start.31 = (bf16[64,512]{1,0:T(8,128)(2,1)S(1)}, bf16[64,512]{1,0:T(8,128)(2,1)S(1)}, u32[]{:S(2)}, u32[]{:S(2)}) collective-permute-start(bf16[64,512]{1,0:T(8,128)(2,1)S(1)} %get-tuple-element.373), channel_id=1, source_target_pairs={{1,0},{2,1},{3,2},{0,3},{5,4},{6,5},{7,6},{4,7},{9,8},{10,9},{11,1... | collective-permute-start | bytes 196616 | tf_op jit(solution)/shard_map/cond/branch_1_fun/ppermute | solution.py:332

commit v2 on v1

--- a/solution.py
+++ b/solution.py
@@ -377,7 +377,7 @@
 
     def body(shifts_hbm, tokens_hbm, table_hbm, *refs):
         outs, refs = refs[:kinds], refs[kinds:]
-        source_ref, rows_ref, flags_ref, *at_refs, shifts_ref, tokens_ref, table_ref, sems = refs
+        rows_ref, flags_ref, *at_refs, shifts_ref, tokens_ref, table_ref, source_ref, sems = refs
         start = Copies(sems)
         shift = start(shifts_hbm, shifts_ref)
         held = start(tokens_hbm, tokens_ref)
@@ -395,17 +395,19 @@
         rows_ref[...] = table_ref[case]
         send_classes(plan, rows_of(plan, table_ref, "send_one", case), source_ref, sizes, which, outs)
 
-    outs = [shape for size in sizes for shape in shapes(size, width)] + shapes([count], width)
+    outs = [shape for size in sizes for shape in shapes(size, width)]
     outs += [pltpu.VMEM(plan.table.shape[1:], F32), pltpu.SMEM((8,), I32)]
     outs += [jax.ShapeDtypeStruct((1,), I32)] * 3
     scratch = [pltpu.SMEM((2,), I32), pltpu.VMEM(tokens.shape, BF16), pltpu.VMEM(plan.table.shape, F32)]
+    scratch += [pltpu.VMEM((count, width), BF16)]
     got = call(body, outs, [shifts, tokens, plan.table], [HBM] * 3, scratch, 3, 1 << 28, 1 << 20)
-    sent, (source, rows, flags, one, two, three) = got[:kinds], got[kinds:]
-    return sent, source, rows, flags, one[0], two[0], three[0]
-
-
-def id_kernel(flags, regions, weights, plan, rows, cols):
+    sent, (rows, flags, one, two, three) = got[:kinds], got[kinds:]
+    return sent, rows, flags, one[0], two[0], three[0]
+
+
+def before_fine(flags, regions, tokens, table, weights, plan):
     _, lat, lon = regions.shape
+    _, rows, cols, width = tokens.shape
     flat_regions = regions.reshape(2 * lat, lon)
     fine, coarse = windowed(rows, cols), natural(rows // 2, cols // 2)
     places = np.asarray(fine + coarse, np.float32)
@@ -416,12 +418,13 @@
     places = np.concatenate([places, is_fine])
     count = len(fine) + len(coarse)
 
-    def body(flags_ref, regions_hbm, places_hbm, *refs):
+    def body(flags_ref, rows_ref, regions_hbm, places_hbm, tokens_hbm, *refs):
         weights_hbm, refs = refs[: len(weights)], refs[len(weights) :]
-        fine_ref, coarse_ref, *refs = refs
-        weight_refs, (regions_ref, places_ref, sems) = refs[: len(weights)], refs[len(weights) :]
+        fine_ref, coarse_ref, x_ref, *refs = refs
+        weight_refs, (regions_ref, places_ref, tokens_ref, sems) = refs[: len(weights)], refs[len(weights) :]
         start = Copies(sems)
         waits = [start(regions_hbm, regions_ref), start(places_hbm, places_ref)]
+        held = start(tokens_hbm, tokens_ref)
         later = [start(src, dst) for src, dst in zip(weights_hbm, weight_refs)]
         for copy in waits:
             copy.wait()
@@ -440,49 +443,71 @@
         picked = select_rows(row, regions_ref[...].astype(F32).astype(BF16))
         ids = jnp.zeros((count, 128), F32)
         for at in range(0, lon, 128):
-            width = min(128, lon - at)
-            lane = lax.broadcasted_iota(I32, (1, width), 1).astype(F32) + float(at)
-            here = jnp.where(lane == col[:, :width], picked[:, at : at + width], 0.0)
+            size = min(128, lon - at)
+            lane = lax.broadcasted_iota(I32, (1, size), 1).astype(F32) + float(at)
+            here = jnp.where(lane == col[:, :size], picked[:, at : at + size], 0.0)
             ids = ids + jnp.sum(here, axis=1, keepdims=True)
         lane = lax.broadcasted_iota(I32, (1, 128), 1).astype(F32)
         hot = jnp.where(lane == ids + wrapped, 1.0, 0.0).astype(BF16)
         fine_ref[...] = hot[: len(fine)]
         coarse_ref[...] = hot[len(fine) :]
+        held.wait()
+        take = columns_of(rows_of(plan, rows_ref, "take_one"), len(fine))
+        x_ref[...] = select_rows(take, flat(tokens_ref)).astype(BF16)
         for copy in later:
             copy.wait()
 
-    outs = shapes([len(fine), len(coarse)], 128) + [pltpu.VMEM(w.shape, BF16) for w in weights]
-    scratch = [pltpu.VMEM(flat_regions.shape, I32), pltpu.VMEM(places.shape, F32)]
-    args = [flags, flat_regions, places, *weights]
-    in_specs = [SMEM] + [HBM] * (2 + len(weights))
-    fine_id, coarse_id, *weights = call(body, outs, args, in_specs, scratch, 2 + len(weights), 1 << 28, 4 << 20)
-    return fine_id, coarse_id, weights
-
-
-def fetch(weights):
-    def body(*refs):
-        sems = refs[-1]
+    outs = shapes([len(fine), len(coarse)], 128) + shapes([len(fine)], width)
+    outs += [pltpu.VMEM(w.shape, BF16) for w in weights]
+    scratch = [pltpu.VMEM(flat_regions.shape, I32), pltpu.VMEM(places.shape, F32), pltpu.VMEM(tokens.shape, BF16)]
+    args = [flags, table, flat_regions, places, tokens, *weights]
+    in_specs = [SMEM, VMEM] + [HBM] * (3 + len(weights))
+    fine_id, coarse_id, x, *weights = call(body, outs, args, in_specs, scratch, 3 + len(weights), 1 << 28, 4 << 20)
+    return fine_id, coarse_id, x, weights
+
+
+CHUNK = 512
+
+
+def before_coarse(fine, table, weights, plan):
+    own, width = fine.shape
+    cuts = [(n, at) for n, w in enumerate(weights) for at in range(0, w.shape[0], CHUNK)]
+
+    def body(rows_ref, fine_hbm, *refs):
+        weights_hbm, refs = refs[: len(weights)], refs[len(weights) :]
+        x_ref, *chunk_refs, fine_ref, sems = refs
         start = Copies(sems)
-        for copy in [start(src, dst) for src, dst in zip(refs[: len(weights)], refs[len(weights) : -1])]:
+        held = start(fine_hbm, fine_ref)
+        later = [start(weights_hbm[n].at[pl.ds(at, CHUNK)], ref) for (n, at), ref in zip(cuts, chunk_refs)]
+        take = columns_of(rows_of(plan, rows_ref, "take_two"), x_ref.shape[0])
+        held.wait()
+        x_ref[...] = select_rows(take, fine_ref[...]).astype(BF16)
+        for copy in later:
             copy.wait()
 
-    outs = [pltpu.VMEM(w.shape, BF16) for w in weights]
+    outs = shapes([own], width) + [pltpu.VMEM((CHUNK, weights[n].shape[1]), BF16) for n, _ in cuts]
     size = sum(2 * w.size for w in weights)
-    return call(body, outs, weights, [HBM] * len(weights), [], len(weights), 0, size)
-
-
-def fine_level(flags, tokens, pieces, key_id, w_qkv, w_proj, rows, plan):
-    count, width = tokens.shape
+    args = [table, fine, *weights]
+    in_specs = [VMEM] + [HBM] * (1 + len(weights))
+    scratch = [pltpu.VMEM(fine.shape, BF16)]
+    x, *chunks = call(body, outs, args, in_specs, scratch, 1 + len(cuts), 1 << 28, size)
+    return x, [[chunk for (m, _), chunk in zip(cuts, chunks) if m == n] for n in range(len(weights))]
+
+
+def fine_level(flags, x_own, pieces, key_id, w_qkv, w_proj, rows, plan):
+    count, width = x_own.shape
     inner = w_proj.shape[0]
     kinds = 3 * len(plan.two)
 
-    def body(flags_ref, tokens_ref, *refs):
+    def body(flags_ref, own_ref, *refs):
         piece_refs, refs = refs[: len(pieces)], refs[len(pieces) :]
-        id_ref, qkv_w_ref, proj_w_ref, rows_ref, out_ref, *refs = refs
-        piece_outs, (source_ref, x_ref, qkv_ref, _) = refs[:kinds], refs[kinds:]
+        id_ref, qkv_w_ref, proj_w_ref, rows_ref, out_hbm, *refs = refs
+        piece_outs, (source_ref, x_ref, qkv_ref, out_ref, sems) = refs[:kinds], refs[kinds:]
+        start = Copies(sems)
+        leave = []
         lay_pieces(piece_refs, plan.one, flags_ref[0], source_ref)
-        take = columns_of(rows_of(plan, rows_ref, "take_one"), count)
-        x = select_rows(take, tokens_ref[...]) + select_rows(take - float(count), source_ref[...])
+        take = columns_of(rows_of(plan, rows_ref, "take_one"), count) - float(count)
+        x = own_ref[...].astype(F32) + select_rows(take, source_ref[...])
         x_ref[...] = x
         normed = layer_norm(x).astype(BF16)
         qkv_ref[...] = jnp.dot(normed, qkv_w_ref[...], preferred_element_type=F32).astype(BF16)
@@ -491,6 +516,7 @@
             at = slice(w * TOK, (w + 1) * TOK)
             out = lax.dot_general(out, proj_w_ref[...], TN, preferred_element_type=F32)
             out_ref[at, :] = (x_ref[at, :] + out).astype(BF16)
+            leave.append(start(out_ref.at[pl.ds(w * TOK, TOK)], out_hbm.at[pl.ds(w * TOK, TOK)]))
 
         attend_windows(
             lambda w, at: qkv_ref[w * TOK : (w + 1) * TOK, at : at + 128],
@@ -500,37 +526,59 @@
             finish,
         )
         send_classes(plan, rows_of(plan, rows_ref, "send_two"), out_ref, plan.two, flags_ref[1], piece_outs)
-
-    outs = shapes([count], width) + [shape for size in plan.two for shape in shapes(size, width)]
+        for copy in leave:
+            copy.wait()
+
+    outs = shapes([count], width, pltpu.HBM) + [shape for size in plan.two for shape in shapes(size, width)]
     scratch = [
         pltpu.VMEM((sum(plan.one[-1]), width), BF16),
         pltpu.VMEM((count, width), F32),
         pltpu.VMEM((count, 3 * inner), BF16),
+        pltpu.VMEM((count, width), BF16),
     ]
-    args = [flags, tokens, *pieces, key_id, w_qkv, w_proj, rows]
-    out, *sent = call(body, outs, args, [SMEM] + [VMEM] * (len(args) - 1), scratch, 1, 3 << 30, 6 << 20)
+    args = [flags, x_own, *pieces, key_id, w_qkv, w_proj, rows]
+    in_specs = [SMEM] + [VMEM] * (len(args) - 1)
+    out, *sent = call(body, outs, args, in_specs, scratch, count // TOK, 3 << 30, 6 << 20)
     return out, sent
 
 
-def coarse_level(flags, fine, pieces, key_id, w_merge, w_qkv, w_proj, rows, plan):
+def coarse_level(flags, fine, x_own, pieces, key_id, weights, rows, plan):
     count = key_id.shape[0]
-    width = w_merge.shape[1]
+    width = weights[0][0].shape[1]
     own, half = fine.shape
-    inner = w_proj.shape[0]
+    inner = CHUNK * len(weights[2])
     kinds = 3 * len(plan.three)
-
-    def body(flags_ref, fine_ref, *refs):
+    chunks = [chunk for w in weights for chunk in w]
+
+    def product(x, refs):
+        parts = [
+            jnp.dot(x[:, n * CHUNK : (n + 1) * CHUNK], ref[...], preferred_element_type=F32)
+            for n, ref in enumerate(refs)
+        ]
+        return functools.reduce(jnp.add, parts)
+
+    def body(flags_ref, fine_hbm, own_ref, *refs):
         piece_refs, refs = refs[: len(pieces)], refs[len(pieces) :]
-        id_ref, merge_ref, qkv_w_ref, proj_w_ref, rows_ref, out_ref, *refs = refs
-        piece_outs, (source_ref, qkv_ref, _) = refs[:kinds], refs[kinds:]
+        chunk_refs, refs = refs[: len(chunks)], refs[len(chunks) :]
+        merge_refs = chunk_refs[: len(weights[0])]
+        qkv_refs = chunk_refs[len(weights[0]) : -len(weights[2])]
+        (proj_w_ref,) = chunk_refs[-len(weights[2]) :]
+        id_ref, rows_ref, out_ref, *refs = refs
+        piece_outs, (source_ref, qkv_ref, fine_ref, sems) = refs[:kinds], refs[kinds:]
+        needs_fine = flags_ref[2] == 1
+
+        @pl.when(needs_fine)
+        def _():
+            pltpu.make_async_copy(fine_hbm, fine_ref, sems.at[0]).start()
+
         lay_pieces(piece_refs, plan.two, flags_ref[1], source_ref)
-        take = columns_of(rows_of(plan, rows_ref, "take_two"), 4 * count)
-        x = select_rows(take, fine_ref[...]) + select_rows(take - float(own), source_ref[...])
+        take = columns_of(rows_of(plan, rows_ref, "take_two"), 4 * count) - float(own)
+        x = own_ref[...].astype(F32) + select_rows(take, source_ref[...])
         x = jnp.concatenate([x[n * count : (n + 1) * count] for n in range(4)], axis=1)
         stacked = layer_norm(x).astype(BF16)
-        merged = jnp.dot(stacked, merge_ref[...], preferred_element_type=F32).astype(BF16).astype(F32)
+        merged = product(stacked, merge_refs).astype(BF16).astype(F32)
         normed = layer_norm(merged).astype(BF16)
-        qkv_ref[...] = jnp.dot(normed, qkv_w_ref[...], preferred_element_type=F32).astype(BF16)
+        qkv_ref[...] = product(normed, qkv_refs).astype(BF16)
 
         def finish(w, out):
             out = lax.dot_general(out, proj_w_ref[...], TN, preferred_element_type=F32)
@@ -549,6 +597,7 @@
                     ref[size : 2 * size, :] = sent[at : at + size, half:]
                     at += size
                 if sum(fine_sizes):
+                    pltpu.make_async_copy(fine_hbm, fine_ref, sems.at[0]).wait()
                     index = columns_of(rows_of(plan, rows_ref, "send_four"), sum(fine_sizes))
                     sent = select_rows(index, fine_ref[...]).astype(BF16)
                     at = 0
@@ -560,27 +609,31 @@
     for sizes, fine_sizes in zip(plan.three, plan.four):
         outs += shapes([2 * n + m for n, m in zip(sizes, fine_sizes)], half)
     scratch = [pltpu.VMEM((sum(plan.two[-1]), half), BF16), pltpu.VMEM((count, 3 * inner), BF16)]
-    args = [flags, fine, *pieces, key_id, w_merge, w_qkv, w_proj, rows]
-    out, *sent = call(body, outs, args, [SMEM] + [VMEM] * (len(args) - 1), scratch, 1, 3 << 30, 12 << 20)
+    scratch += [pltpu.VMEM(fine.shape, BF16)]
+    args = [flags, fine, x_own, *pieces, *chunks, key_id, rows]
+    in_specs = [SMEM, HBM] + [VMEM] * (len(args) - 2)
+    out, *sent = call(body, outs, args, in_specs, scratch, 1, 3 << 30, 12 << 20)
     return out, sent
 
 
 def fine_output(flags, fine, pieces, rows, plan, block_rows, block_cols, partial):
     own, width = fine.shape
 
-    def body(flags_ref, fine_ref, *refs):
-        piece_refs, (rows_ref, out_ref, source_ref, _) = refs[: len(pieces)], refs[len(pieces) :]
+    def body(flags_ref, fine_hbm, *refs):
+        piece_refs, (rows_ref, out_ref, source_ref, fine_ref, sems) = refs[: len(pieces)], refs[len(pieces) :]
+        held = Copies(sems)(fine_hbm, fine_ref)
         lay_pieces(piece_refs, plan.two, flags_ref[1], source_ref)
         take = columns_of(rows_of(plan, rows_ref, "fine_out"), own)
+        held.wait()
         out = select_rows(take, fine_ref[...]) + select_rows(take - float(own), source_ref[...])
         out_ref[...] = (out if partial else out.reshape(out_ref.shape)).astype(BF16)
 
     outs = [jax.ShapeDtypeStruct((2, block_rows, block_cols, width), BF16)]
     if partial:
         outs = shapes([own], width)
-    scratch = [pltpu.VMEM((sum(plan.two[-1]), width), BF16)]
+    scratch = [pltpu.VMEM((sum(plan.two[-1]), width), BF16), pltpu.VMEM(fine.shape, BF16)]
     args = [flags, fine, *pieces, rows]
-    return call(body, outs, args, [SMEM] + [VMEM] * (len(args) - 1), scratch, 1, 1 << 30, 4 << 20)[0]
+    return call(body, outs, args, [SMEM, HBM] + [VMEM] * (len(args) - 2), scratch, 1, 1 << 30, 4 << 20)[0]
 
 
 def coarse_output(coarse, got, rows, which, plan, block_rows, block_cols, part=None):
@@ -617,12 +670,11 @@
     _, rows, cols, _ = tokens.shape
     plan = Plan(rows, cols)
 
-    def first(which, sign, sent, flags, regions, weights):
-        got = exchange_class(sent, which, sign)
-        return got, id_kernel(flags, regions, weights, plan, rows, cols)
-
-    def second(which, sign, sent, weights):
-        return exchange_class(sent, which, sign), fetch(weights)
+    def first(which, sign, sent, *args):
+        return exchange_class(sent, which, sign), before_fine(*args, plan)
+
+    def second(which, sign, sent, *args):
+        return exchange_class(sent, which, sign), before_coarse(*args, plan)
 
     def third(which, sign, sent, flags, fine, pieces, coarse, table):
         got = exchange(sent[3 * which : 3 * which + 3], sign)
@@ -637,14 +689,14 @@
     def branches(stage, pairs):
         return [functools.partial(stage, which, sign) for which, sign in pairs]
 
-    sent, source, table, flags, one, two, three = first_pieces(shifts, tokens, plan)
-    got, (fine_id, coarse_id, weights) = choose(
-        one, branches(first, plan.one_branches), sent, flags, regions, [fine_qkv, fine_proj]
+    sent, table, flags, one, two, three = first_pieces(shifts, tokens, plan)
+    got, (fine_id, coarse_id, x, weights) = choose(
+        one, branches(first, plan.one_branches), sent, flags, regions, tokens, table, [fine_qkv, fine_proj]
     )
-    fine, sent = fine_level(flags, source, got, fine_id, *weights, table, plan)
+    fine, sent = fine_level(flags, x, got, fine_id, *weights, table, plan)
     weights = [merge_weight, coarse_qkv, coarse_proj]
-    got, weights = choose(two, branches(second, plan.two_branches), sent, weights)
-    coarse, sent = coarse_level(flags, fine, got, coarse_id, *weights, table, plan)
+    got, (x, weights) = choose(two, branches(second, plan.two_branches), sent, fine, table, weights)
+    coarse, sent = coarse_level(flags, fine, x, got, coarse_id, weights, table, plan)
     return choose(three, branches(third, plan.three_branches), sent, flags, fine, got, coarse, table)
 
 

time: 57.3 us -> 68.3 us (1.19)
  local copies, waits for them, and re-layouts: 11.5 us -> 22.1 us
  waiting for transfers between devices: 3.9 us -> 1.61 us
  Pallas kernels: 25.9 us -> 27.1 us
  starting transfers between devices: 12.2 us -> 13.2 us
    cond x4 -> x22, local copies, waits for them, and re-layouts: 3.72 us -> 9.14 us
    unnamed x12 -> x28, local copies, waits for them, and re-layouts: 7.81 us -> 13 us
    ppermute x3, waiting for transfers between devices: 3.88 us -> 1.59 us  [exchange(): both = lax.ppermute(both, ('lat', 'lon'), pairs)]
    pallas_call x7, Pallas kernels: 24.4 us -> 25.7 us  [call(): pl.pallas_call(body, out_shape=outs, in_specs=in_specs, out_specs=out_spe...]
  transfers between devices with their start and end apart: 9 -> 9, of which waited for: 1 -> 2; matrix products, arithmetic and copies ran while one was open for 0% -> 0% of each run, Pallas kernels for 17% -> 16%
where the time goes in v2:
time: 68.3 us; the launch traced here: 67.1 us
  Pallas kernels  27.1 us (40%)
  local copies, waits for them, and re-layouts  22.1 us (32%)
  starting transfers between devices  13.2 us (19%)
  loops' own time  2.23 us (3%)
  waiting for transfers between devices  1.61 us (2%)
  between operations  0.85 us (1%)
    pallas_call x7, Pallas kernels, call(): pl.pallas_call(body, out_shape=outs, in_specs=in_specs, out_specs=out_spe...  25.7 us
    unnamed x28, local copies, waits for them, and re-layouts  13 us
    cond x22, local copies, waits for them, and re-layouts  9.14 us
    ppermute x3, starting transfers between devices, exchange(): col = lax.ppermute(col, 'lon', [((j + sign) % lon, j) for j in range(lon)])  6.72 us
    ppermute x3, starting transfers between devices, exchange(): both = lax.ppermute(both, ('lat', 'lon'), pairs)  4.26 us
    another operation x3, loops' own time, choose(): lax.cond_p.bind(index, *flat_args, branches=tuple((closed(branch) for bra...  2.23 us
    ppermute x3, starting transfers between devices, exchange(): row = lax.ppermute(row, 'lat', [((i + sign) % lat, i) for i in range(lat)])  2.18 us
    ppermute x3, waiting for transfers between devices, exchange(): both = lax.ppermute(both, ('lat', 'lon'), pairs)  1.59 us
  transfers between devices with their start and end apart: 9, of which 2 were waited for; matrix products, arithmetic and copies ran while one was open for 0% of the time, Pallas kernels for 16%

profile of v2, /device:TPU:0, one launch (start us, length us, event | category | flops | bytes accessed | tf_op | source)
XLA Modules:
  0.0 67.1 jit_solution(11097507437451338275)
XLA Ops:
  0.6 2.0 %shard_map.110 = (bf16[48,512]{1,0:T(8,128)(2,1)S(1)}, bf16[48,512]{1,0:T(8,128)(2,1)S(1)}, bf16[16,512]{1,0:T(8,128)(2,1)S(1)}, bf16[112,512]{1,0:T(8,128)(2,1)...) custom-call(s32[2]{0:T(128)} %shifts_hbm.1, ...), custom_call_target="tpu_custom_call" | custom-call | flops 268435456 | bytes 1048576 | tf_op jit(solution)/shard_map/pallas_call | solution.py:264
  2.6 10.7 %conditional.3 = (bf16[48,512]{1,0:T(8,128)(2,1)}, bf16[48,512]{1,0:T(8,128)(2,1)}, bf16[16,512]{1,0:T(8,128)(2,1)}, bf16[112,512]{1,0:T(8,128)(2,1)}, bf16[112,...) conditional(s32[]{:T(128)} %bitcast.8, ...), branch_computations={%region_0.0_spmd, %region_1.0_spmd, %region_2.0_spmd, %region_3.0_... | conditional | flops 268435456 | bytes 5456108 | solution.py:357
  3.3 0.5 collective-permute-start
  3.8 2.6 %collective-permute-start.1 = (bf16[48,512]{1,0:T(8,128)(2,1)S(1)}, bf16[48,512]{1,0:T(8,128)(2,1)}, u32[]{:S(2)}, u32[]{:S(2)}) collective-permute-start(bf16[48,512]{1,0:T(8,128)(2,1)S(1)} %get-tuple-element.249), channel_id=1, source_target_pairs={{3,0},{0,1},{1,2},{2,3},{7,4},{4,5},{5,6},{6,7},{11,8},{8,9},{9,10... | collective-permute-start | bytes 147464 | tf_op jit(solution)/shard_map/cond/branch_0_fun/ppermute | solution.py:332
  6.4 2.4 %collective-permute-start.2 = (bf16[16,512]{1,0:T(8,128)(2,1)S(1)}, bf16[16,512]{1,0:T(8,128)(2,1)}, u32[]{:S(2)}, u32[]{:S(2)}) collective-permute-start(bf16[16,512]{1,0:T(8,128)(2,1)S(1)} %get-tuple-element.250), channel_id=1, source_target_pairs={{31,0},{28,1},{29,2},{30,3},{3,4},{0,5},{1,6},{2,7},{7,8},{4,9},{5... | collective-permute-start | bytes 49160 | tf_op jit(solution)/shard_map/cond/branch_0_fun/ppermute | solution.py:333
  8.9 0.7 %branch_0_fun.7 = (bf16[112,512]{1,0:T(8,128)(2,1)}, bf16[112,512]{1,0:T(8,128)(2,1)}, bf16[48,512]{1,0:T(8,128)(2,1)}) custom-call(), custom_call_target="tpu_custom_call" | custom-call | tf_op jit(solution)/shard_map/cond/branch_0_fun/pallas_call | solution.py:340
  9.6 2.2 %branch_0_fun.8 = (bf16[576,128]{1,0:T(8,128)(2,1)S(1)}, bf16[144,128]{1,0:T(8,128)(2,1)S(1)}, bf16[576,512]{1,0:T(8,128)(2,1)S(1)}, bf16[512,1536]{1,0:T(8,128)(2,1)S(1)}, bf16[512,512]{1,0:T(8,128)(2,1)S(1)}) custom-call(s32[8]{0:T(128)S(4)} %get-tuple-element.254.flags_ref, f32[32,128]{1,0:T(8,128)S(1)} %get-tuple-element.255.rows_ref, ...), custom_call_target="tpu_custom_call" | custom-call | flops 268435456 | bytes 4194304 | tf_op jit(solution)/shard_map/cond/branch_0_fun/pallas_call | solution.py:264
  11.8 0.6 copy-done.55
  12.4 0.9 %collective-permute-done.2 = bf16[16,512]{1,0:T(8,128)(2,1)} collective-permute-done((bf16[16,512]{1,0:T(8,128)(2,1)S(1)}, bf16[16,512]{1,0:T(8,128)(2,1)}, u32[]{:S(2)}, u32[]{:S(2)}) %collective-permute-start.2) | collective-permute-done | bytes 16416 | tf_op jit(solution)/shard_map/cond/branch_0_fun/ppermute | solution.py:333
  13.3 8.0 %shard_map.111 = (bf16[576,512]{1,0:T(8,128)(2,1)}, bf16[48,512]{1,0:T(8,128)(2,1)S(1)}, bf16[48,512]{1,0:T(8,128)(2,1)}, bf16[16,512]{1,0:T(8,128)(2,1)S(1)}, b...) custom-call(s32[8]{0:T(128)S(4)} %get-tuple-element.535.flags_ref, ...), custom_call_target="tpu_custom_call" | custom-call | flops 3221225472 | bytes 6291456 | tf_op jit(solution)/shard_map/pallas_call | solution.py:264
  21.3 0.6 copy-done.36
  22.0 0.7 copy-done.37
  22.6 0.6 copy-done.38
  23.3 0.6 copy-done.39
  23.9 15.0 %conditional.4 = (bf16[48,512]{1,0:T(8,128)(2,1)}, bf16[48,512]{1,0:T(8,128)(2,1)}, bf16[16,512]{1,0:T(8,128)(2,1)}, bf16[128,512]{1,0:T(8,128)(2,1)}, bf16[128,...) conditional(s32[]{:T(128)} %bitcast.9, ...), branch_computations={%region_4.0_spmd, %region_5.0_spmd, %region_6.0_spmd, %region_7.0_... | conditional | flops 268435456 | bytes 36045308 | solution.py:357
  24.7 0.1 collective-permute-start.21
  24.8 0.8 %collective-permute-start.22 = (bf16[160,512]{1,0:T(8,128)(2,1)S(1)}, bf16[160,512]{1,0:T(8,128)(2,1)}, u32[]{:S(2)}, u32[]{:S(2)}) collective-permute-start(bf16[160,512]{1,0:T(8,128)(2,1)S(1)} %get-tuple-element.389), channel_id=1, source_target_pairs={{3,0},{0,1},{1,2},{2,3},{7,4},{4,5},{5,6},{6,7},{11,8},{8,9},{9,10... | collective-permute-start | bytes 491528 | tf_op jit(solution)/shard_map/cond/branch_3_fun/ppermute | solution.py:332
  25.6 1.1 %collective-permute-start.23 = (bf16[112,512]{1,0:T(8,128)(2,1)}, bf16[112,512]{1,0:T(8,128)(2,1)}, u32[]{:S(2)}, u32[]{:S(2)}) collective-permute-start(bf16[112,512]{1,0:T(8,128)(2,1)} %get-tuple-element.390), channel_id=1, source_target_pairs={{31,0},{28,1},{29,2},{30,3},{3,4},{0,5},{1,6},{2,7},{7,8},{4,9},{5... | collective-permute-start | bytes 344072 | tf_op jit(solution)/shard_map/cond/branch_3_fun/ppermute | solution.py:333
  26.8 0.6 copy-done.43
  27.4 0.6 copy-done.52
  28.0 0.6 copy-done.63
  28.6 0.7 %branch_3_fun.8 = (bf16[128,512]{1,0:T(8,128)(2,1)}, bf16[128,512]{1,0:T(8,128)(2,1)}, bf16[48,512]{1,0:T(8,128)(2,1)}) custom-call(), custom_call_target="tpu_custom_call" | custom-call | tf_op jit(solution)/shard_map/cond/branch_3_fun/pallas_call | solution.py:340
  29.3 3.6 %branch_3_fun.9 = (bf16[576,512]{1,0:T(8,128)(2,1)S(1)}, bf16[512,1024]{1,0:T(8,128)(2,1)S(1)}, bf16[512,1024]{1,0:T(8,128)(2,1)S(1)}, bf16[512,1024]{1,0:T(8,12...) custom-call(f32[32,128]{1,0:T(8,128)S(1)} %get-tuple-element.391.row, ...), custom_call_target="tpu_custom_call" | custom-call | flops 268435456 | bytes 8388608 | tf_op jit(solution)/shard_map/cond/branch_3_fun/pallas_call | solution.py:264
  33.0 1.1 %copy-done.3 = bf16[512,1536]{1,0:T(8,128)(2,1)} copy-done((bf16[512,1536]{1,0:T(8,128)(2,1)}, bf16[512,1536]{1,0:T(8,128)(2,1)S(1)}, u32[]{:S(2)}) %copy-start.3) | copy-done | bytes 1572888 | tf_op jit(solution)/shard_map/cond
  34.1 1.0 %copy-done.9 = bf16[512,1024]{1,0:T(8,128)(2,1)} copy-done((bf16[512,1024]{1,0:T(8,128)(2,1)}, bf16[512,1024]{1,0:T(8,128)(2,1)S(1)}, u32[]{:S(2)}) %copy-start.9) | copy-done | bytes 1048600 | tf_op jit(solution)/shard_map/cond
  35.1 1.0 %copy-done.15 = bf16[512,1024]{1,0:T(8,128)(2,1)} copy-done((bf16[512,1024]{1,0:T(8,128)(2,1)}, bf16[512,1024]{1,0:T(8,128)(2,1)S(1)}, u32[]{:S(2)}) %copy-start.15) | copy-done | bytes 1048600 | tf_op jit(solution)/shard_map/cond
  36.1 1.0 %copy-done.21 = bf16[512,1024]{1,0:T(8,128)(2,1)} copy-done((bf16[512,1024]{1,0:T(8,128)(2,1)}, bf16[512,1024]{1,0:T(8,128)(2,1)S(1)}, u32[]{:S(2)}) %copy-start.21) | copy-done | bytes 1048600 | tf_op jit(solution)/shard_map/cond
  37.1 1.0 %copy-done.27 = bf16[512,1024]{1,0:T(8,128)(2,1)} copy-done((bf16[512,1024]{1,0:T(8,128)(2,1)}, bf16[512,1024]{1,0:T(8,128)(2,1)S(1)}, u32[]{:S(2)}) %copy-start.27) | copy-done | bytes 1048600 | tf_op jit(solution)/shard_map/cond
  38.1 0.8 %copy-done.33 = bf16[576,512]{1,0:T(8,128)(2,1)} copy-done((bf16[576,512]{1,0:T(8,128)(2,1)}, bf16[576,512]{1,0:T(8,128)(2,1)S(1)}, u32[]{:S(2)}) %copy-start.33) | copy-done | bytes 589848 | tf_op jit(solution)/shard_map/cond
  38.9 1.4 %copy-done.5 = bf16[512,1536]{1,0:T(8,128)(2,1)S(1)} copy-done((bf16[512,1536]{1,0:T(8,128)(2,1)S(1)}, bf16[512,1536]{1,0:T(8,128)(2,1)}, u32[]{:S(2)}) %copy-start.5) | copy-done | bytes 1572888
  40.3 1.2 %copy-done.11 = bf16[512,1024]{1,0:T(8,128)(2,1)S(1)} copy-done((bf16[512,1024]{1,0:T(8,128)(2,1)S(1)}, bf16[512,1024]{1,0:T(8,128)(2,1)}, u32[]{:S(2)}) %copy-start.11) | copy-done | bytes 1048600
  41.6 1.2 %copy-done.17 = bf16[512,1024]{1,0:T(8,128)(2,1)S(1)} copy-done((bf16[512,1024]{1,0:T(8,128)(2,1)S(1)}, bf16[512,1024]{1,0:T(8,128)(2,1)}, u32[]{:S(2)}) %copy-start.17) | copy-done | bytes 1048600
  42.8 1.2 %copy-done.23 = bf16[512,1024]{1,0:T(8,128)(2,1)S(1)} copy-done((bf16[512,1024]{1,0:T(8,128)(2,1)S(1)}, bf16[512,1024]{1,0:T(8,128)(2,1)}, u32[]{:S(2)}) %copy-start.23) | copy-done | bytes 1048600
  44.0 1.2 %copy-done.29 = bf16[512,1024]{1,0:T(8,128)(2,1)S(1)} copy-done((bf16[512,1024]{1,0:T(8,128)(2,1)S(1)}, bf16[512,1024]{1,0:T(8,128)(2,1)}, u32[]{:S(2)}) %copy-start.29) | copy-done | bytes 1048600
  45.2 1.1 %copy-done.35 = bf16[576,512]{1,0:T(8,128)(2,1)S(1)} copy-done((bf16[576,512]{1,0:T(8,128)(2,1)S(1)}, bf16[576,512]{1,0:T(8,128)(2,1)}, u32[]{:S(2)}) %copy-start.35) | copy-done | bytes 589848
  46.3 0.8 %copy-done.45 = bf16[48,512]{1,0:T(8,128)(2,1)S(1)} copy-done((bf16[48,512]{1,0:T(8,128)(2,1)S(1)}, bf16[48,512]{1,0:T(8,128)(2,1)}, u32[]{:S(2)}) %copy-start.45) | copy-done | bytes 49176
  47.1 0.8 %copy-done.54 = bf16[48,512]{1,0:T(8,128)(2,1)S(1)} copy-done((bf16[48,512]{1,0:T(8,128)(2,1)S(1)}, bf16[48,512]{1,0:T(8,128)(2,1)}, u32[]{:S(2)}) %copy-start.54) | copy-done | bytes 49176
  47.9 0.8 %copy-done.59 = bf16[144,128]{1,0:T(8,128)(2,1)S(1)} copy-done((bf16[144,128]{1,0:T(8,128)(2,1)S(1)}, bf16[144,128]{1,0:T(8,128)(2,1)}, u32[]{:S(2)}) %copy-start.59) | copy-done | bytes 36888
  48.7 0.7 %copy-done.65 = bf16[16,512]{1,0:T(8,128)(2,1)S(1)} copy-done((bf16[16,512]{1,0:T(8,128)(2,1)S(1)}, bf16[16,512]{1,0:T(8,128)(2,1)}, u32[]{:S(2)}) %copy-start.65) | copy-done | bytes 16408
  49.4 5.3 %shard_map.112 = (bf16[144,1024]{1,0:T(8,128)(2,1)S(1)}, bf16[64,512]{1,0:T(8,128)(2,1)S(1)}, bf16[64,512]{1,0:T(8,128)(2,1)S(1)}, bf16[32,512]{1,0:T(8,128)(2,1...) custom-call(s32[8]{0:T(128)S(4)} %get-tuple-element.535.flags_ref, ...), custom_call_target="tpu_custom_call" | custom-call | flops 3221225472 | bytes 12582912 | tf_op jit(solution)/shard_map/pallas_call | solution.py:264
  54.7 12.3 %conditional.5 = (bf16[2,12,24,512]{3,2,1,0:T(8,128)(2,1)}, bf16[2,6,12,1024]{3,0,2,1:T(2,128)(2,1)}) conditional(s32[]{:T(128)} %bitcast.7, (s32[8]{0:T(128)S(4)}, bf16[576,512]{1,0:T(8,128)(2,1)}, bf16[48,512]{1,0:T(8,128)(2,1)}, bf16[48,512]{1,0:T(8,128)(2,1)S(1)}, bf16[16,512]{1,0:T(8,128)(2,1)S(1)}, ...), branch_computations={%region_9.0_spmd, %region_10.0_spmd, %region_11.0_spmd} | conditional | flops 1342177280 | bytes 7078052 | solution.py:357
  55.4 1.6 %collective-permute-start.33 = (bf16[144,512]{1,0:T(8,128)(2,1)S(1)}, bf16[144,512]{1,0:T(8,128)(2,1)S(1)}, u32[]{:S(2)}, u32[]{:S(2)}) collective-permute-start(bf16[144,512]{1,0:T(8,128)(2,1)S(1)} %get-tuple-element.459), channel_id=1, source_target_pairs={{4,0},{8,4},{12,8},{16,12},{20,16},{24,20},{28,24},{0,28},{5,1},{9... | collective-permute-start | bytes 442376 | tf_op jit(solution)/shard_map/cond/branch_2_fun/ppermute | solution.py:334
  57.0 3.2 %collective-permute-start.34 = (bf16[144,512]{1,0:T(8,128)(2,1)S(1)}, bf16[144,512]{1,0:T(8,128)(2,1)S(1)}, u32[]{:S(2)}, u32[]{:S(2)}) collective-permute-start(bf16[144,512]{1,0:T(8,128)(2,1)S(1)} %get-tuple-element.460), channel_id=1, source_target_pairs={{1,0},{2,1},{3,2},{0,3},{5,4},{6,5},{7,6},{4,7},{9,8},{10,9},{11,1... | collective-permute-start | bytes 442376 | tf_op jit(solution)/shard_map/cond/branch_2_fun/ppermute | solution.py:332
  60.2 0.7 %collective-permute-start.35 = (bf16[112,512]{1,0:T(8,128)(2,1)S(1)}, bf16[112,512]{1,0:T(8,128)(2,1)S(1)}, u32[]{:S(2)}, u32[]{:S(2)}) collective-permute-start(bf16[112,512]{1,0:T(8,128)(2,1)S(1)} %get-tuple-element.461), channel_id=1, source_target_pairs={{5,0},{6,1},{7,2},{4,3},{9,4},{10,5},{11,6},{8,7},{13,8},{14,9},{1... | collective-permute-start | bytes 344072 | tf_op jit(solution)/shard_map/cond/branch_2_fun/ppermute | solution.py:333
  60.9 0.8 %copy-done.48 = bf16[48,512]{1,0:T(8,128)(2,1)S(1)} copy-done((bf16[48,512]{1,0:T(8,128)(2,1)S(1)}, bf16[48,512]{1,0:T(8,128)(2,1)}, u32[]{:S(2)}) %copy-start.48) | copy-done | bytes 49176 | tf_op jit(solution)/shard_map/cond
  61.7 3.2 %branch_2_fun.12.refs_3_ = bf16[576,512]{1,0:T(8,128)(2,1)S(1)} custom-call(s32[8]{0:T(128)S(4)} %get-tuple-element.462.flags_ref, bf16[576,512]{1,0:T(8,128)(2,1)} %get-tuple-element.463.fine_hbm, bf16[48,512]{1,0:T(8,128)(2,1)S(1)} %copy-done.48, bf16[48,512]{1,0:T(8,128)(2,1)S(1)} %get-tuple-element.465.refs_1_, ...), custom_call_target="tpu_custom_call" | custom-call | flops 1073741824 | bytes 4194304 | tf_op jit(solution)/shard_map/cond/branch_2_fun/pallas_call | solution.py:264
  64.9 0.7 collective-permute-done.35.refs_2_
  65.6 1.3 %branch_2_fun.13 = (bf16[6,12,2,1024]{3,2,1,0:T(2,128)(2,1)}, bf16[2,12,24,512]{3,2,1,0:T(8,128)(2,1)}) custom-call(bf16[144,1024]{1,0:T(8,128)(2,1)S(1)} %get-tuple-element.458.coarse_ref, bf16[144,512]{1,0:T(8,128)(2,1)S(1)} %collective-permute-done.33.refs_0_, bf16[144,512]{1,0:T(8,128)(2,1)S(1)} %collective-permute-done.34.refs_1_, ...), custom_call_target="tpu_custom_call" | custom-call | flops 268435456 | bytes 1048576 | tf_op jit(solution)/shard_map/cond/branch_2_fun/pallas_call | solution.py:264
  (33 shorter events, 0.1 us)
Async XLA Ops:
  3.3 10.0 %collective-permute-start = (bf16[48,512]{1,0:T(8,128)(2,1)S(1)}, bf16[48,512]{1,0:T(8,128)(2,1)}, u32[]{:S(2)}, u32[]{:S(2)}) collective-permute-start(bf16[48,512]{1,0:T(8,128)(2,1)S(1)} %get-tuple-element.248), channel_id=1, source_target_pairs={{28,0},{0,4},{4,8},{8,12},{12,16},{16,20},{20,24},{24,28},{29,1},{... | collective-permute-start | bytes 147464 | tf_op jit(solution)/shard_map/cond/branch_0_fun/ppermute | solution.py:334
  3.8 9.5 %collective-permute-start.1 = (bf16[48,512]{1,0:T(8,128)(2,1)S(1)}, bf16[48,512]{1,0:T(8,128)(2,1)}, u32[]{:S(2)}, u32[]{:S(2)}) collective-permute-start(bf16[48,512]{1,0:T(8,128)(2,1)S(1)} %get-tuple-element.249), channel_id=1, source_target_pairs={{3,0},{0,1},{1,2},{2,3},{7,4},{4,5},{5,6},{6,7},{11,8},{8,9},{9,10... | collective-permute-start | bytes 147464 | tf_op jit(solution)/shard_map/cond/branch_0_fun/ppermute | solution.py:332
  6.4 6.9 %collective-permute-start.2 = (bf16[16,512]{1,0:T(8,128)(2,1)S(1)}, bf16[16,512]{1,0:T(8,128)(2,1)}, u32[]{:S(2)}, u32[]{:S(2)}) collective-permute-start(bf16[16,512]{1,0:T(8,128)(2,1)S(1)} %get-tuple-element.250), channel_id=1, source_target_pairs={{31,0},{28,1},{29,2},{30,3},{3,4},{0,5},{1,6},{2,7},{7,8},{4,9},{5... | collective-permute-start | bytes 49160 | tf_op jit(solution)/shard_map/cond/branch_0_fun/ppermute | solution.py:333
  11.7 0.6 copy-start.55
  21.3 0.7 copy-start.36
  22.0 0.7 copy-start.37
  22.6 0.6 copy-start.38
  23.3 0.6 copy-start.39
  24.7 14.2 %collective-permute-start.21 = (bf16[160,512]{1,0:T(8,128)(2,1)S(1)}, bf16[160,512]{1,0:T(8,128)(2,1)}, u32[]{:S(2)}, u32[]{:S(2)}) collective-permute-start(bf16[160,512]{1,0:T(8,128)(2,1)S(1)} %get-tuple-element.388), channel_id=1, source_target_pairs={{28,0},{0,4},{4,8},{8,12},{12,16},{16,20},{20,24},{24,28},{29,1},{... | collective-permute-start | bytes 491528 | tf_op jit(solution)/shard_map/cond/branch_3_fun/ppermute | solution.py:334
  24.8 14.1 %collective-permute-start.22 = (bf16[160,512]{1,0:T(8,128)(2,1)S(1)}, bf16[160,512]{1,0:T(8,128)(2,1)}, u32[]{:S(2)}, u32[]{:S(2)}) collective-permute-start(bf16[160,512]{1,0:T(8,128)(2,1)S(1)} %get-tuple-element.389), channel_id=1, source_target_pairs={{3,0},{0,1},{1,2},{2,3},{7,4},{4,5},{5,6},{6,7},{11,8},{8,9},{9,10... | collective-permute-start | bytes 491528 | tf_op jit(solution)/shard_map/cond/branch_3_fun/ppermute | solution.py:332
  25.6 13.3 %collective-permute-start.23 = (bf16[112,512]{1,0:T(8,128)(2,1)}, bf16[112,512]{1,0:T(8,128)(2,1)}, u32[]{:S(2)}, u32[]{:S(2)}) collective-permute-start(bf16[112,512]{1,0:T(8,128)(2,1)} %get-tuple-element.390), channel_id=1, source_target_pairs={{31,0},{28,1},{29,2},{30,3},{3,4},{0,5},{1,6},{2,7},{7,8},{4,9},{5... | collective-permute-start | bytes 344072 | tf_op jit(solution)/shard_map/cond/branch_3_fun/ppermute | solution.py:333
  26.8 0.6 copy-start.43
  27.4 0.6 copy-start.52
  28.0 0.6 copy-start.63
  33.0 1.2 %copy-start.3 = (bf16[512,1536]{1,0:T(8,128)(2,1)}, bf16[512,1536]{1,0:T(8,128)(2,1)S(1)}, u32[]{:S(2)}) copy-start(bf16[512,1536]{1,0:T(8,128)(2,1)S(1)} %get-tuple-element.702) | copy-start | bytes 4718596 | tf_op jit(solution)/shard_map/cond
  34.1 1.0 %copy-start.9 = (bf16[512,1024]{1,0:T(8,128)(2,1)}, bf16[512,1024]{1,0:T(8,128)(2,1)S(1)}, u32[]{:S(2)}) copy-start(bf16[512,1024]{1,0:T(8,128)(2,1)S(1)} %get-tuple-element.698) | copy-start | bytes 3145732 | tf_op jit(solution)/shard_map/cond
  35.1 1.0 %copy-start.15 = (bf16[512,1024]{1,0:T(8,128)(2,1)}, bf16[512,1024]{1,0:T(8,128)(2,1)S(1)}, u32[]{:S(2)}) copy-start(bf16[512,1024]{1,0:T(8,128)(2,1)S(1)} %get-tuple-element.699) | copy-start | bytes 3145732 | tf_op jit(solution)/shard_map/cond
  36.1 1.0 %copy-start.21 = (bf16[512,1024]{1,0:T(8,128)(2,1)}, bf16[512,1024]{1,0:T(8,128)(2,1)S(1)}, u32[]{:S(2)}) copy-start(bf16[512,1024]{1,0:T(8,128)(2,1)S(1)} %get-tuple-element.700) | copy-start | bytes 3145732 | tf_op jit(solution)/shard_map/cond
  37.1 1.0 %copy-start.27 = (bf16[512,1024]{1,0:T(8,128)(2,1)}, bf16[512,1024]{1,0:T(8,128)(2,1)S(1)}, u32[]{:S(2)}) copy-start(bf16[512,1024]{1,0:T(8,128)(2,1)S(1)} %get-tuple-element.703) | copy-start | bytes 3145732 | tf_op jit(solution)/shard_map/cond
  38.1 0.8 %copy-start.33 = (bf16[576,512]{1,0:T(8,128)(2,1)}, bf16[576,512]{1,0:T(8,128)(2,1)S(1)}, u32[]{:S(2)}) copy-start(bf16[576,512]{1,0:T(8,128)(2,1)S(1)} %get-tuple-element.696) | copy-start | bytes 1769476 | tf_op jit(solution)/shard_map/cond
  38.9 1.4 %copy-start.5 = (bf16[512,1536]{1,0:T(8,128)(2,1)S(1)}, bf16[512,1536]{1,0:T(8,128)(2,1)}, u32[]{:S(2)}) copy-start(bf16[512,1536]{1,0:T(8,128)(2,1)} %get-tuple-element.580.refs_14_) | copy-start | bytes 4718596
  40.3 1.2 %copy-start.11 = (bf16[512,1024]{1,0:T(8,128)(2,1)S(1)}, bf16[512,1024]{1,0:T(8,128)(2,1)}, u32[]{:S(2)}) copy-start(bf16[512,1024]{1,0:T(8,128)(2,1)} %get-tuple-element.576.refs_10_) | copy-start | bytes 3145732
  41.6 1.2 %copy-start.17 = (bf16[512,1024]{1,0:T(8,128)(2,1)S(1)}, bf16[512,1024]{1,0:T(8,128)(2,1)}, u32[]{:S(2)}) copy-start(bf16[512,1024]{1,0:T(8,128)(2,1)} %get-tuple-element.577.refs_11_) | copy-start | bytes 3145732
  42.8 1.2 %copy-start.23 = (bf16[512,1024]{1,0:T(8,128)(2,1)S(1)}, bf16[512,1024]{1,0:T(8,128)(2,1)}, u32[]{:S(2)}) copy-start(bf16[512,1024]{1,0:T(8,128)(2,1)} %get-tuple-element.578.refs_12_) | copy-start | bytes 3145732
  44.0 1.2 %copy-start.29 = (bf16[512,1024]{1,0:T(8,128)(2,1)S(1)}, bf16[512,1024]{1,0:T(8,128)(2,1)}, u32[]{:S(2)}) copy-start(bf16[512,1024]{1,0:T(8,128)(2,1)} %get-tuple-element.581.refs_15_) | copy-start | bytes 3145732
  45.2 1.1 %copy-start.35 = (bf16[576,512]{1,0:T(8,128)(2,1)S(1)}, bf16[576,512]{1,0:T(8,128)(2,1)}, u32[]{:S(2)}) copy-start(bf16[576,512]{1,0:T(8,128)(2,1)} %get-tuple-element.574.own_ref) | copy-start | bytes 1769476
  46.3 0.8 %copy-start.45 = (bf16[48,512]{1,0:T(8,128)(2,1)S(1)}, bf16[48,512]{1,0:T(8,128)(2,1)}, u32[]{:S(2)}) copy-start(bf16[48,512]{1,0:T(8,128)(2,1)} %get-tuple-element.565.refs_0_) | copy-start | bytes 147460
  47.1 0.8 %copy-start.54 = (bf16[48,512]{1,0:T(8,128)(2,1)S(1)}, bf16[48,512]{1,0:T(8,128)(2,1)}, u32[]{:S(2)}) copy-start(bf16[48,512]{1,0:T(8,128)(2,1)} %get-tuple-element.566.refs_1_) | copy-start | bytes 147460
  47.9 0.8 %copy-start.59 = (bf16[144,128]{1,0:T(8,128)(2,1)S(1)}, bf16[144,128]{1,0:T(8,128)(2,1)}, u32[]{:S(2)}) copy-start(bf16[144,128]{1,0:T(8,128)(2,1)} %get-tuple-element.582.refs_16_) | copy-start | bytes 110596
  48.7 0.7 %copy-start.65 = (bf16[16,512]{1,0:T(8,128)(2,1)S(1)}, bf16[16,512]{1,0:T(8,128)(2,1)}, u32[]{:S(2)}) copy-start(bf16[16,512]{1,0:T(8,128)(2,1)} %get-tuple-element.567.refs_2_) | copy-start | bytes 49156
  55.4 10.3 %collective-permute-start.33 = (bf16[144,512]{1,0:T(8,128)(2,1)S(1)}, bf16[144,512]{1,0:T(8,128)(2,1)S(1)}, u32[]{:S(2)}, u32[]{:S(2)}) collective-permute-start(bf16[144,512]{1,0:T(8,128)(2,1)S(1)} %get-tuple-element.459), channel_id=1, source_target_pairs={{4,0},{8,4},{12,8},{16,12},{20,16},{24,20},{28,24},{0,28},{5,1},{9... | collective-permute-start | bytes 442376 | tf_op jit(solution)/shard_map/cond/branch_2_fun/ppermute | solution.py:334
  57.0 8.7 %collective-permute-start.34 = (bf16[144,512]{1,0:T(8,128)(2,1)S(1)}, bf16[144,512]{1,0:T(8,128)(2,1)S(1)}, u32[]{:S(2)}, u32[]{:S(2)}) collective-permute-start(bf16[144,512]{1,0:T(8,128)(2,1)S(1)} %get-tuple-element.460), channel_id=1, source_target_pairs={{1,0},{2,1},{3,2},{0,3},{5,4},{6,5},{7,6},{4,7},{9,8},{10,9},{11,1... | collective-permute-start | bytes 442376 | tf_op jit(solution)/shard_map/cond/branch_2_fun/ppermute | solution.py:332
  60.2 5.4 %collective-permute-start.35 = (bf16[112,512]{1,0:T(8,128)(2,1)S(1)}, bf16[112,512]{1,0:T(8,128)(2,1)S(1)}, u32[]{:S(2)}, u32[]{:S(2)}) collective-permute-start(bf16[112,512]{1,0:T(8,128)(2,1)S(1)} %get-tuple-element.461), channel_id=1, source_target_pairs={{5,0},{6,1},{7,2},{4,3},{9,4},{10,5},{11,6},{8,7},{13,8},{14,9},{1... | collective-permute-start | bytes 344072 | tf_op jit(solution)/shard_map/cond/branch_2_fun/ppermute | solution.py:333
  60.9 0.8 %copy-start.48 = (bf16[48,512]{1,0:T(8,128)(2,1)S(1)}, bf16[48,512]{1,0:T(8,128)(2,1)}, u32[]{:S(2)}) copy-start(bf16[48,512]{1,0:T(8,128)(2,1)} %get-tuple-element.464.refs_0_) | copy-start | bytes 147460 | tf_op jit(solution)/shard_map/cond

commit v3 on v2

--- a/solution.py
+++ b/solution.py
@@ -255,7 +255,7 @@
 SMEM = pl.BlockSpec(memory_space=pltpu.SMEM)
 
 
-def call(body, outs, args, in_specs, scratch, copies, flops, moved_bytes, vmem=32):
+def call(body, outs, args, in_specs, scratch, copies, flops, moved_bytes, vmem=8):
     args = [
         pltpu.with_memory_space_constraint(arg, spec.memory_space) for arg, spec in zip(args, in_specs, strict=True)
     ]
@@ -336,10 +336,8 @@
 
 
 def unused(like):
-    outs = [pltpu.VMEM(x.shape, x.dtype) for x in like]
-    return pl.pallas_call(
-        lambda *refs: None, out_shape=outs, out_specs=[pl.BlockSpec(memory_space=pltpu.VMEM)] * len(outs)
-    )()
+    outs = [jax.ShapeDtypeStruct(x.shape, x.dtype) for x in like]
+    return pl.pallas_call(lambda *refs: None, out_shape=outs, out_specs=[ANY] * len(outs))()
 
 
 def choose(index, branches, *args):
@@ -538,7 +536,7 @@
     ]
     args = [flags, x_own, *pieces, key_id, w_qkv, w_proj, rows]
     in_specs = [SMEM] + [VMEM] * (len(args) - 1)
-    out, *sent = call(body, outs, args, in_specs, scratch, count // TOK, 3 << 30, 6 << 20)
+    out, *sent = call(body, outs, args, in_specs, scratch, count // TOK, 3 << 30, 6 << 20, 14)
     return out, sent
 
 
@@ -612,7 +610,7 @@
     scratch += [pltpu.VMEM(fine.shape, BF16)]
     args = [flags, fine, x_own, *pieces, *chunks, key_id, rows]
     in_specs = [SMEM, HBM] + [VMEM] * (len(args) - 2)
-    out, *sent = call(body, outs, args, in_specs, scratch, 1, 3 << 30, 12 << 20)
+    out, *sent = call(body, outs, args, in_specs, scratch, 1, 3 << 30, 12 << 20, 14)
     return out, sent
 
 

time: 68.3 us -> 66.3 us (0.971)
  local copies, waits for them, and re-layouts: 22.1 us -> 20.5 us
  waiting for transfers between devices: 1.61 us -> 2.99 us
  Pallas kernels: 27.1 us -> 25.9 us
    cond x22 -> x14, local copies, waits for them, and re-layouts: 9.14 us -> 6.36 us
    ppermute x3, starting transfers between devices: 2.18 us -> 3.74 us  [exchange(): row = lax.ppermute(row, 'lat', [((i + sign) % lat, i) for i in range(lat)])]
    pallas_call x3, Pallas kernels: 1.45 us -> 0.01 us  [unused(): pl.pallas_call(lambda *refs: None, out_shape=outs, out_specs=[ANY] * len(...]
    ppermute x3, waiting for transfers between devices: 1.59 us -> 2.97 us  [exchange(): both = lax.ppermute(both, ('lat', 'lon'), pairs)]
    unnamed x28 -> x32, local copies, waits for them, and re-layouts: 13 us -> 14.2 us
    ppermute x3, starting transfers between devices: 6.72 us -> 5.88 us  [exchange(): col = lax.ppermute(col, 'lon', [((j + sign) % lon, j) for j in range(lon)])]
    ppermute x3, starting transfers between devices: 4.26 us -> 3.47 us  [exchange(): both = lax.ppermute(both, ('lat', 'lon'), pairs)]
  transfers between devices with their start and end apart: 9 -> 9, of which waited for: 2 -> 2; matrix products, arithmetic and copies ran while one was open for 0% -> 0% of each run, Pallas kernels for 16% -> 15%
where the time goes in v3:
time: 66.3 us; the launch traced here: 65.7 us
  Pallas kernels  25.9 us (39%)
  local copies, waits for them, and re-layouts  20.5 us (31%)
  starting transfers between devices  13.1 us (20%)
  waiting for transfers between devices  2.99 us (5%)
  loops' own time  2.32 us (3%)
  between operations  0.84 us (1%)
    pallas_call x7, Pallas kernels, call(): pl.pallas_call(body, out_shape=outs, in_specs=in_specs, out_specs=out_spe...  25.9 us
    unnamed x32, local copies, waits for them, and re-layouts  14.2 us
    cond x14, local copies, waits for them, and re-layouts  6.36 us
    ppermute x3, starting transfers between devices, exchange(): col = lax.ppermute(col, 'lon', [((j + sign) % lon, j) for j in range(lon)])  5.88 us
    ppermute x3, starting transfers between devices, exchange(): row = lax.ppermute(row, 'lat', [((i + sign) % lat, i) for i in range(lat)])  3.74 us
    ppermute x3, starting transfers between devices, exchange(): both = lax.ppermute(both, ('lat', 'lon'), pairs)  3.47 us
    ppermute x3, waiting for transfers between devices, exchange(): both = lax.ppermute(both, ('lat', 'lon'), pairs)  2.97 us
    another operation x3, loops' own time, choose(): lax.cond_p.bind(index, *flat_args, branches=tuple((closed(branch) for bra...  2.32 us
  transfers between devices with their start and end apart: 9, of which 2 were waited for; matrix products, arithmetic and copies ran while one was open for 0% of the time, Pallas kernels for 15%

profile of v3, /device:TPU:0, one launch (start us, length us, event | category | flops | bytes accessed | tf_op | source)
XLA Modules:
  0.0 65.7 jit_solution(9009613955545478022)
XLA Ops:
  0.6 2.1 %shard_map.110 = (bf16[48,512]{1,0:T(8,128)(2,1)S(1)}, bf16[48,512]{1,0:T(8,128)(2,1)S(1)}, bf16[16,512]{1,0:T(8,128)(2,1)S(1)}, bf16[112,512]{1,0:T(8,128)(2,1)...) custom-call(s32[2]{0:T(128)} %shifts_hbm.1, ...), custom_call_target="tpu_custom_call" | custom-call | flops 268435456 | bytes 1048576 | tf_op jit(solution)/shard_map/pallas_call | solution.py:264
  2.7 11.5 %conditional.3 = (bf16[48,512]{1,0:T(8,128)(2,1)}, bf16[48,512]{1,0:T(8,128)(2,1)}, bf16[16,512]{1,0:T(8,128)(2,1)}, bf16[112,512]{1,0:T(8,128)(2,1)}, bf16[112,...) conditional(s32[]{:T(128)} %bitcast.8, ...), branch_computations={%region_0.0_spmd, %region_1.0_spmd, %region_2.0_spmd, %region_3.0_... | conditional | flops 268435456 | bytes 5456108 | solution.py:355
  3.4 3.4 %collective-permute-start.9 = (bf16[112,512]{1,0:T(8,128)(2,1)S(1)}, bf16[112,512]{1,0:T(8,128)(2,1)}, u32[]{:S(2)}, u32[]{:S(2)}) collective-permute-start(bf16[112,512]{1,0:T(8,128)(2,1)S(1)} %get-tuple-element.302), channel_id=1, source_target_pairs={{4,0},{8,4},{12,8},{16,12},{20,16},{24,20},{28,24},{0,28},{5,1},{9... | collective-permute-start | bytes 344072 | tf_op jit(solution)/shard_map/cond/branch_3_fun/ppermute | solution.py:334
  6.8 3.6 %collective-permute-start.10 = (bf16[112,512]{1,0:T(8,128)(2,1)S(1)}, bf16[112,512]{1,0:T(8,128)(2,1)}, u32[]{:S(2)}, u32[]{:S(2)}) collective-permute-start(bf16[112,512]{1,0:T(8,128)(2,1)S(1)} %get-tuple-element.303), channel_id=1, source_target_pairs={{1,0},{2,1},{3,2},{0,3},{5,4},{6,5},{7,6},{4,7},{9,8},{10,9},{11,1... | collective-permute-start | bytes 344072 | tf_op jit(solution)/shard_map/cond/branch_3_fun/ppermute | solution.py:332
  10.4 0.3 collective-permute-start.11
  10.7 2.2 %branch_3_fun.6 = (bf16[576,128]{1,0:T(8,128)(2,1)S(1)}, bf16[144,128]{1,0:T(8,128)(2,1)S(1)}, bf16[576,512]{1,0:T(8,128)(2,1)S(1)}, bf16[512,1536]{1,0:T(8,128)(2,1)S(1)}, bf16[512,512]{1,0:T(8,128)(2,1)S(1)}) custom-call(s32[8]{0:T(128)S(4)} %get-tuple-element.305.flags_ref, f32[32,128]{1,0:T(8,128)S(1)} %get-tuple-element.306.rows_ref, ...), custom_call_target="tpu_custom_call" | custom-call | flops 268435456 | bytes 4194304 | tf_op jit(solution)/shard_map/cond/branch_3_fun/pallas_call | solution.py:264
  12.9 0.6 copy-done.49
  13.5 0.7 %collective-permute-done.11 = bf16[48,512]{1,0:T(8,128)(2,1)} collective-permute-done((bf16[48,512]{1,0:T(8,128)(2,1)S(1)}, bf16[48,512]{1,0:T(8,128)(2,1)}, u32[]{:S(2)}, u32[]{:S(2)}) %collective-permute-start.11) | collective-permute-done | bytes 49184 | tf_op jit(solution)/shard_map/cond/branch_3_fun/ppermute | solution.py:333
  14.2 0.0 collective-permute-done.9
  14.2 8.0 %shard_map.111 = (bf16[576,512]{1,0:T(8,128)(2,1)}, bf16[48,512]{1,0:T(8,128)(2,1)S(1)}, bf16[48,512]{1,0:T(8,128)(2,1)S(1)}, bf16[16,512]{1,0:T(8,128)(2,1)}, b...) custom-call(s32[8]{0:T(128)S(4)} %get-tuple-element.535.flags_ref, ...), custom_call_target="tpu_custom_call" | custom-call | flops 3221225472 | bytes 6291456 | tf_op jit(solution)/shard_map/pallas_call | solution.py:264
  22.2 0.0 copy-start.36
  22.3 0.7 copy-done.36
  22.9 0.7 %copy-done.37 = bf16[160,512]{1,0:T(8,128)(2,1)} copy-done((bf16[160,512]{1,0:T(8,128)(2,1)}, bf16[160,512]{1,0:T(8,128)(2,1)S(1)}, u32[]{:S(2)}) %copy-start.37) | copy-done | bytes 163864
  23.6 0.6 copy-done.38
  24.2 0.7 %copy-done.39 = bf16[128,512]{1,0:T(8,128)(2,1)} copy-done((bf16[128,512]{1,0:T(8,128)(2,1)}, bf16[128,512]{1,0:T(8,128)(2,1)S(1)}, u32[]{:S(2)}) %copy-start.39) | copy-done | bytes 131096
  24.9 0.6 copy-done.40
  25.5 0.6 copy-done.41
  26.2 13.7 %conditional.4 = (bf16[48,512]{1,0:T(8,128)(2,1)}, bf16[48,512]{1,0:T(8,128)(2,1)}, bf16[16,512]{1,0:T(8,128)(2,1)}, bf16[128,512]{1,0:T(8,128)(2,1)}, bf16[128,...) conditional(s32[]{:T(128)} %bitcast.9, ...), branch_computations={%region_4.0_spmd, %region_5.0_spmd, %region_6.0_spmd, %region_7.0_... | conditional | flops 268435456 | bytes 33489320 | solution.py:355
  27.0 0.1 collective-permute-start.21
  27.1 1.1 %collective-permute-start.22 = (bf16[160,512]{1,0:T(8,128)(2,1)}, bf16[160,512]{1,0:T(8,128)(2,1)}, u32[]{:S(2)}, u32[]{:S(2)}) collective-permute-start(bf16[160,512]{1,0:T(8,128)(2,1)} %get-tuple-element.389), channel_id=1, source_target_pairs={{3,0},{0,1},{1,2},{2,3},{7,4},{4,5},{5,6},{6,7},{11,8},{8,9},{9,10... | collective-permute-start | bytes 491528 | tf_op jit(solution)/shard_map/cond/branch_3_fun/ppermute | solution.py:332
  28.2 0.0 collective-permute-start.23
  28.2 3.6 %branch_3_fun.9 = (bf16[576,512]{1,0:T(8,128)(2,1)S(1)}, bf16[512,1024]{1,0:T(8,128)(2,1)S(1)}, bf16[512,1024]{1,0:T(8,128)(2,1)S(1)}, bf16[512,1024]{1,0:T(8,12...) custom-call(f32[32,128]{1,0:T(8,128)S(1)} %get-tuple-element.391.row, ...), custom_call_target="tpu_custom_call" | custom-call | flops 268435456 | bytes 8388608 | tf_op jit(solution)/shard_map/cond/branch_3_fun/pallas_call | solution.py:264
  31.8 1.0 %copy-done.3 = bf16[512,1024]{1,0:T(8,128)(2,1)} copy-done((bf16[512,1024]{1,0:T(8,128)(2,1)}, bf16[512,1024]{1,0:T(8,128)(2,1)S(1)}, u32[]{:S(2)}) %copy-start.3) | copy-done | bytes 1048600 | tf_op jit(solution)/shard_map/cond
  32.8 1.0 %copy-done.9 = bf16[512,1024]{1,0:T(8,128)(2,1)} copy-done((bf16[512,1024]{1,0:T(8,128)(2,1)}, bf16[512,1024]{1,0:T(8,128)(2,1)S(1)}, u32[]{:S(2)}) %copy-start.9) | copy-done | bytes 1048600 | tf_op jit(solution)/shard_map/cond
  33.8 1.0 %copy-done.15 = bf16[512,1024]{1,0:T(8,128)(2,1)} copy-done((bf16[512,1024]{1,0:T(8,128)(2,1)}, bf16[512,1024]{1,0:T(8,128)(2,1)S(1)}, u32[]{:S(2)}) %copy-start.15) | copy-done | bytes 1048600 | tf_op jit(solution)/shard_map/cond
  34.8 1.0 %copy-done.21 = bf16[512,1024]{1,0:T(8,128)(2,1)} copy-done((bf16[512,1024]{1,0:T(8,128)(2,1)}, bf16[512,1024]{1,0:T(8,128)(2,1)S(1)}, u32[]{:S(2)}) %copy-start.21) | copy-done | bytes 1048600 | tf_op jit(solution)/shard_map/cond
  35.8 1.0 %copy-done.27 = bf16[512,1024]{1,0:T(8,128)(2,1)} copy-done((bf16[512,1024]{1,0:T(8,128)(2,1)}, bf16[512,1024]{1,0:T(8,128)(2,1)S(1)}, u32[]{:S(2)}) %copy-start.27) | copy-done | bytes 1048600 | tf_op jit(solution)/shard_map/cond
  36.8 0.8 %copy-done.33 = bf16[576,512]{1,0:T(8,128)(2,1)} copy-done((bf16[576,512]{1,0:T(8,128)(2,1)}, bf16[576,512]{1,0:T(8,128)(2,1)S(1)}, u32[]{:S(2)}) %copy-start.33) | copy-done | bytes 589848 | tf_op jit(solution)/shard_map/cond
  37.6 2.2 %collective-permute-done.23 = bf16[112,512]{1,0:T(8,128)(2,1)} collective-permute-done((bf16[112,512]{1,0:T(8,128)(2,1)}, bf16[112,512]{1,0:T(8,128)(2,1)}, u32[]{:S(2)}, u32[]{:S(2)}) %collective-permute-start.23) | collective-permute-done | bytes 114720 | tf_op jit(solution)/shard_map/cond/branch_3_fun/ppermute | solution.py:333
  39.9 1.2 %copy-done.5 = bf16[512,1024]{1,0:T(8,128)(2,1)S(1)} copy-done((bf16[512,1024]{1,0:T(8,128)(2,1)S(1)}, bf16[512,1024]{1,0:T(8,128)(2,1)}, u32[]{:S(2)}) %copy-start.5) | copy-done | bytes 1048600
  41.1 1.2 %copy-done.11 = bf16[512,1024]{1,0:T(8,128)(2,1)S(1)} copy-done((bf16[512,1024]{1,0:T(8,128)(2,1)S(1)}, bf16[512,1024]{1,0:T(8,128)(2,1)}, u32[]{:S(2)}) %copy-start.11) | copy-done | bytes 1048600
  42.3 1.2 %copy-done.17 = bf16[512,1024]{1,0:T(8,128)(2,1)S(1)} copy-done((bf16[512,1024]{1,0:T(8,128)(2,1)S(1)}, bf16[512,1024]{1,0:T(8,128)(2,1)}, u32[]{:S(2)}) %copy-start.17) | copy-done | bytes 1048600
  43.5 1.2 %copy-done.23 = bf16[512,1024]{1,0:T(8,128)(2,1)S(1)} copy-done((bf16[512,1024]{1,0:T(8,128)(2,1)S(1)}, bf16[512,1024]{1,0:T(8,128)(2,1)}, u32[]{:S(2)}) %copy-start.23) | copy-done | bytes 1048600
  44.8 1.2 %copy-done.29 = bf16[512,1024]{1,0:T(8,128)(2,1)S(1)} copy-done((bf16[512,1024]{1,0:T(8,128)(2,1)S(1)}, bf16[512,1024]{1,0:T(8,128)(2,1)}, u32[]{:S(2)}) %copy-start.29) | copy-done | bytes 1048600
  46.0 1.1 %copy-done.35 = bf16[576,512]{1,0:T(8,128)(2,1)S(1)} copy-done((bf16[576,512]{1,0:T(8,128)(2,1)S(1)}, bf16[576,512]{1,0:T(8,128)(2,1)}, u32[]{:S(2)}) %copy-start.35) | copy-done | bytes 589848
  47.0 0.8 %copy-done.43 = bf16[48,512]{1,0:T(8,128)(2,1)S(1)} copy-done((bf16[48,512]{1,0:T(8,128)(2,1)S(1)}, bf16[48,512]{1,0:T(8,128)(2,1)}, u32[]{:S(2)}) %copy-start.43) | copy-done | bytes 49176
  47.8 0.8 %copy-done.45 = bf16[48,512]{1,0:T(8,128)(2,1)S(1)} copy-done((bf16[48,512]{1,0:T(8,128)(2,1)S(1)}, bf16[48,512]{1,0:T(8,128)(2,1)}, u32[]{:S(2)}) %copy-start.45) | copy-done | bytes 49176
  48.6 0.8 %copy-done.50 = bf16[144,128]{1,0:T(8,128)(2,1)S(1)} copy-done((bf16[144,128]{1,0:T(8,128)(2,1)S(1)}, bf16[144,128]{1,0:T(8,128)(2,1)}, u32[]{:S(2)}) %copy-start.50) | copy-done | bytes 36888
  49.4 0.7 %copy-done.52 = bf16[16,512]{1,0:T(8,128)(2,1)S(1)} copy-done((bf16[16,512]{1,0:T(8,128)(2,1)S(1)}, bf16[16,512]{1,0:T(8,128)(2,1)}, u32[]{:S(2)}) %copy-start.52) | copy-done | bytes 16408
  50.1 5.0 %shard_map.112 = (bf16[144,1024]{1,0:T(8,128)(2,1)S(1)}, bf16[64,512]{1,0:T(8,128)(2,1)S(1)}, bf16[64,512]{1,0:T(8,128)(2,1)S(1)}, bf16[32,512]{1,0:T(8,128)(2,1...) custom-call(s32[8]{0:T(128)S(4)} %get-tuple-element.535.flags_ref, ...), custom_call_target="tpu_custom_call" | custom-call | flops 3221225472 | bytes 12582912 | tf_op jit(solution)/shard_map/pallas_call | solution.py:264
  55.1 10.4 %conditional.5 = (bf16[2,12,24,512]{3,2,1,0:T(8,128)(2,1)}, bf16[2,6,12,1024]{3,0,2,1:T(2,128)(2,1)}) conditional(s32[]{:T(128)} %bitcast.7, (s32[8]{0:T(128)S(4)}, bf16[576,512]{1,0:T(8,128)(2,1)}, bf16[48,512]{1,0:T(8,128)(2,1)S(1)}, bf16[48,512]{1,0:T(8,128)(2,1)S(1)}, bf16[16,512]{1,0:T(8,128)(2,1)S(1)}, ...), branch_computations={%region_9.0_spmd, %region_10.0_spmd, %region_11.0_spmd} | conditional | flops 1342177280 | bytes 6881416 | solution.py:355
  55.8 3.2 %collective-permute-start.32 = (bf16[32,512]{1,0:T(8,128)(2,1)S(1)}, bf16[32,512]{1,0:T(8,128)(2,1)S(1)}, u32[]{:S(2)}, u32[]{:S(2)}) collective-permute-start(bf16[32,512]{1,0:T(8,128)(2,1)S(1)} %get-tuple-element.457), channel_id=1, source_target_pairs={{5,0},{6,1},{7,2},{4,3},{9,4},{10,5},{11,6},{8,7},{13,8},{14,9},{1... | collective-permute-start | bytes 98312 | tf_op jit(solution)/shard_map/cond/branch_1_fun/ppermute | solution.py:333
  59.0 0.3 collective-permute-start.30
  59.3 1.2 %collective-permute-start.31 = (bf16[64,512]{1,0:T(8,128)(2,1)S(1)}, bf16[64,512]{1,0:T(8,128)(2,1)S(1)}, u32[]{:S(2)}, u32[]{:S(2)}) collective-permute-start(bf16[64,512]{1,0:T(8,128)(2,1)S(1)} %get-tuple-element.456), channel_id=1, source_target_pairs={{1,0},{2,1},{3,2},{0,3},{5,4},{6,5},{7,6},{4,7},{9,8},{10,9},{11,1... | collective-permute-start | bytes 196616 | tf_op jit(solution)/shard_map/cond/branch_1_fun/ppermute | solution.py:332
  60.5 4.0 %branch_1_fun.12 = bf16[2,12,24,512]{3,2,1,0:T(8,128)(2,1)} custom-call(s32[8]{0:T(128)S(4)} %get-tuple-element.442.flags_ref, bf16[576,512]{1,0:T(8,128)(2,1)} %get-tuple-element.443.fine_hbm, bf16[48,512]{1,0:T(8,128)(2,1)S(1)} %get-tuple-element.444.refs_0_, bf16[48,512]{1,0:T(8,128)(2,1)S(1)} %get-tuple-element.445.refs_1_, ...), custom_call_target="tpu_custom_call" | custom-call | flops 1073741824 | bytes 4194304 | tf_op jit(solution)/shard_map/cond/branch_1_fun/pallas_call | solution.py:264
  64.5 0.0 collective-permute-done.30.refs_0_
  64.5 0.0 collective-permute-done.31.refs_1_
  64.5 1.0 %branch_1_fun.13 = bf16[6,12,2,1024]{3,2,1,0:T(2,128)(2,1)} custom-call(bf16[144,1024]{1,0:T(8,128)(2,1)S(1)} %get-tuple-element.454.coarse_ref, bf16[64,512]{1,0:T(8,128)(2,1)S(1)} %collective-permute-done.30.refs_0_, bf16[64,512]{1,0:T(8,128)(2,1)S(1)} %collective-permute-done.31.refs_1_, bf16[32,512]{1,0:T(8,128)(2,1)S(1)} %collective-permute-done.32.refs_2_, ...), custom_call_target="tpu_custom_call" | custom-call | flops 268435456 | bytes 1048576 | tf_op jit(solution)/shard_map/cond/branch_1_fun/pallas_call | solution.py:264
  (29 shorter events, 0.0 us)
Async XLA Ops:
  3.4 10.8 %collective-permute-start.9 = (bf16[112,512]{1,0:T(8,128)(2,1)S(1)}, bf16[112,512]{1,0:T(8,128)(2,1)}, u32[]{:S(2)}, u32[]{:S(2)}) collective-permute-start(bf16[112,512]{1,0:T(8,128)(2,1)S(1)} %get-tuple-element.302), channel_id=1, source_target_pairs={{4,0},{8,4},{12,8},{16,12},{20,16},{24,20},{28,24},{0,28},{5,1},{9... | collective-permute-start | bytes 344072 | tf_op jit(solution)/shard_map/cond/branch_3_fun/ppermute | solution.py:334
  6.8 7.4 %collective-permute-start.10 = (bf16[112,512]{1,0:T(8,128)(2,1)S(1)}, bf16[112,512]{1,0:T(8,128)(2,1)}, u32[]{:S(2)}, u32[]{:S(2)}) collective-permute-start(bf16[112,512]{1,0:T(8,128)(2,1)S(1)} %get-tuple-element.303), channel_id=1, source_target_pairs={{1,0},{2,1},{3,2},{0,3},{5,4},{6,5},{7,6},{4,7},{9,8},{10,9},{11,1... | collective-permute-start | bytes 344072 | tf_op jit(solution)/shard_map/cond/branch_3_fun/ppermute | solution.py:332
  10.4 3.8 %collective-permute-start.11 = (bf16[48,512]{1,0:T(8,128)(2,1)S(1)}, bf16[48,512]{1,0:T(8,128)(2,1)}, u32[]{:S(2)}, u32[]{:S(2)}) collective-permute-start(bf16[48,512]{1,0:T(8,128)(2,1)S(1)} %get-tuple-element.304), channel_id=1, source_target_pairs={{5,0},{6,1},{7,2},{4,3},{9,4},{10,5},{11,6},{8,7},{13,8},{14,9},{1... | collective-permute-start | bytes 147464 | tf_op jit(solution)/shard_map/cond/branch_3_fun/ppermute | solution.py:333
  12.9 0.6 copy-start.49
  22.2 0.7 %copy-start.36 = (bf16[160,512]{1,0:T(8,128)(2,1)}, bf16[160,512]{1,0:T(8,128)(2,1)S(1)}, u32[]{:S(2)}) copy-start(bf16[160,512]{1,0:T(8,128)(2,1)S(1)} %get-tuple-element.562) | copy-start | bytes 491524
  22.9 0.7 %copy-start.37 = (bf16[160,512]{1,0:T(8,128)(2,1)}, bf16[160,512]{1,0:T(8,128)(2,1)S(1)}, u32[]{:S(2)}) copy-start(bf16[160,512]{1,0:T(8,128)(2,1)S(1)} %get-tuple-element.563) | copy-start | bytes 491524
  23.6 0.7 copy-start.38
  24.2 0.7 %copy-start.39 = (bf16[128,512]{1,0:T(8,128)(2,1)}, bf16[128,512]{1,0:T(8,128)(2,1)S(1)}, u32[]{:S(2)}) copy-start(bf16[128,512]{1,0:T(8,128)(2,1)S(1)} %get-tuple-element.560) | copy-start | bytes 393220
  24.9 0.6 copy-start.40
  25.5 0.6 copy-start.41
  27.0 12.8 %collective-permute-start.21 = (bf16[160,512]{1,0:T(8,128)(2,1)}, bf16[160,512]{1,0:T(8,128)(2,1)}, u32[]{:S(2)}, u32[]{:S(2)}) collective-permute-start(bf16[160,512]{1,0:T(8,128)(2,1)} %get-tuple-element.388), channel_id=1, source_target_pairs={{28,0},{0,4},{4,8},{8,12},{12,16},{16,20},{20,24},{24,28},{29,1},{... | collective-permute-start | bytes 491528 | tf_op jit(solution)/shard_map/cond/branch_3_fun/ppermute | solution.py:334
  27.1 12.8 %collective-permute-start.22 = (bf16[160,512]{1,0:T(8,128)(2,1)}, bf16[160,512]{1,0:T(8,128)(2,1)}, u32[]{:S(2)}, u32[]{:S(2)}) collective-permute-start(bf16[160,512]{1,0:T(8,128)(2,1)} %get-tuple-element.389), channel_id=1, source_target_pairs={{3,0},{0,1},{1,2},{2,3},{7,4},{4,5},{5,6},{6,7},{11,8},{8,9},{9,10... | collective-permute-start | bytes 491528 | tf_op jit(solution)/shard_map/cond/branch_3_fun/ppermute | solution.py:332
  28.2 11.7 %collective-permute-start.23 = (bf16[112,512]{1,0:T(8,128)(2,1)}, bf16[112,512]{1,0:T(8,128)(2,1)}, u32[]{:S(2)}, u32[]{:S(2)}) collective-permute-start(bf16[112,512]{1,0:T(8,128)(2,1)} %get-tuple-element.390), channel_id=1, source_target_pairs={{31,0},{28,1},{29,2},{30,3},{3,4},{0,5},{1,6},{2,7},{7,8},{4,9},{5... | collective-permute-start | bytes 344072 | tf_op jit(solution)/shard_map/cond/branch_3_fun/ppermute | solution.py:333
  31.8 1.0 %copy-start.3 = (bf16[512,1024]{1,0:T(8,128)(2,1)}, bf16[512,1024]{1,0:T(8,128)(2,1)S(1)}, u32[]{:S(2)}) copy-start(bf16[512,1024]{1,0:T(8,128)(2,1)S(1)} %get-tuple-element.697) | copy-start | bytes 3145732 | tf_op jit(solution)/shard_map/cond
  32.8 1.0 %copy-start.9 = (bf16[512,1024]{1,0:T(8,128)(2,1)}, bf16[512,1024]{1,0:T(8,128)(2,1)S(1)}, u32[]{:S(2)}) copy-start(bf16[512,1024]{1,0:T(8,128)(2,1)S(1)} %get-tuple-element.698) | copy-start | bytes 3145732 | tf_op jit(solution)/shard_map/cond
  33.8 1.0 %copy-start.15 = (bf16[512,1024]{1,0:T(8,128)(2,1)}, bf16[512,1024]{1,0:T(8,128)(2,1)S(1)}, u32[]{:S(2)}) copy-start(bf16[512,1024]{1,0:T(8,128)(2,1)S(1)} %get-tuple-element.699) | copy-start | bytes 3145732 | tf_op jit(solution)/shard_map/cond
  34.8 1.0 %copy-start.21 = (bf16[512,1024]{1,0:T(8,128)(2,1)}, bf16[512,1024]{1,0:T(8,128)(2,1)S(1)}, u32[]{:S(2)}) copy-start(bf16[512,1024]{1,0:T(8,128)(2,1)S(1)} %get-tuple-element.700) | copy-start | bytes 3145732 | tf_op jit(solution)/shard_map/cond
  35.8 1.0 %copy-start.27 = (bf16[512,1024]{1,0:T(8,128)(2,1)}, bf16[512,1024]{1,0:T(8,128)(2,1)S(1)}, u32[]{:S(2)}) copy-start(bf16[512,1024]{1,0:T(8,128)(2,1)S(1)} %get-tuple-element.703) | copy-start | bytes 3145732 | tf_op jit(solution)/shard_map/cond
  36.8 0.8 %copy-start.33 = (bf16[576,512]{1,0:T(8,128)(2,1)}, bf16[576,512]{1,0:T(8,128)(2,1)S(1)}, u32[]{:S(2)}) copy-start(bf16[576,512]{1,0:T(8,128)(2,1)S(1)} %get-tuple-element.696) | copy-start | bytes 1769476 | tf_op jit(solution)/shard_map/cond
  39.8 1.2 %copy-start.5 = (bf16[512,1024]{1,0:T(8,128)(2,1)S(1)}, bf16[512,1024]{1,0:T(8,128)(2,1)}, u32[]{:S(2)}) copy-start(bf16[512,1024]{1,0:T(8,128)(2,1)} %get-tuple-element.575.refs_9_) | copy-start | bytes 3145732
  41.1 1.2 %copy-start.11 = (bf16[512,1024]{1,0:T(8,128)(2,1)S(1)}, bf16[512,1024]{1,0:T(8,128)(2,1)}, u32[]{:S(2)}) copy-start(bf16[512,1024]{1,0:T(8,128)(2,1)} %get-tuple-element.576.refs_10_) | copy-start | bytes 3145732
  42.3 1.2 %copy-start.17 = (bf16[512,1024]{1,0:T(8,128)(2,1)S(1)}, bf16[512,1024]{1,0:T(8,128)(2,1)}, u32[]{:S(2)}) copy-start(bf16[512,1024]{1,0:T(8,128)(2,1)} %get-tuple-element.577.refs_11_) | copy-start | bytes 3145732
  43.5 1.2 %copy-start.23 = (bf16[512,1024]{1,0:T(8,128)(2,1)S(1)}, bf16[512,1024]{1,0:T(8,128)(2,1)}, u32[]{:S(2)}) copy-start(bf16[512,1024]{1,0:T(8,128)(2,1)} %get-tuple-element.578.refs_12_) | copy-start | bytes 3145732
  44.8 1.2 %copy-start.29 = (bf16[512,1024]{1,0:T(8,128)(2,1)S(1)}, bf16[512,1024]{1,0:T(8,128)(2,1)}, u32[]{:S(2)}) copy-start(bf16[512,1024]{1,0:T(8,128)(2,1)} %get-tuple-element.581.refs_15_) | copy-start | bytes 3145732
  46.0 1.1 %copy-start.35 = (bf16[576,512]{1,0:T(8,128)(2,1)S(1)}, bf16[576,512]{1,0:T(8,128)(2,1)}, u32[]{:S(2)}) copy-start(bf16[576,512]{1,0:T(8,128)(2,1)} %get-tuple-element.574.own_ref) | copy-start | bytes 1769476
  47.0 0.8 %copy-start.43 = (bf16[48,512]{1,0:T(8,128)(2,1)S(1)}, bf16[48,512]{1,0:T(8,128)(2,1)}, u32[]{:S(2)}) copy-start(bf16[48,512]{1,0:T(8,128)(2,1)} %get-tuple-element.565.refs_0_) | copy-start | bytes 147460
  47.8 0.8 %copy-start.45 = (bf16[48,512]{1,0:T(8,128)(2,1)S(1)}, bf16[48,512]{1,0:T(8,128)(2,1)}, u32[]{:S(2)}) copy-start(bf16[48,512]{1,0:T(8,128)(2,1)} %get-tuple-element.566.refs_1_) | copy-start | bytes 147460
  48.6 0.8 %copy-start.50 = (bf16[144,128]{1,0:T(8,128)(2,1)S(1)}, bf16[144,128]{1,0:T(8,128)(2,1)}, u32[]{:S(2)}) copy-start(bf16[144,128]{1,0:T(8,128)(2,1)} %get-tuple-element.582.refs_16_) | copy-start | bytes 110596
  49.4 0.7 %copy-start.52 = (bf16[16,512]{1,0:T(8,128)(2,1)S(1)}, bf16[16,512]{1,0:T(8,128)(2,1)}, u32[]{:S(2)}) copy-start(bf16[16,512]{1,0:T(8,128)(2,1)} %get-tuple-element.567.refs_2_) | copy-start | bytes 49156
  55.8 8.7 %collective-permute-start.32 = (bf16[32,512]{1,0:T(8,128)(2,1)S(1)}, bf16[32,512]{1,0:T(8,128)(2,1)S(1)}, u32[]{:S(2)}, u32[]{:S(2)}) collective-permute-start(bf16[32,512]{1,0:T(8,128)(2,1)S(1)} %get-tuple-element.457), channel_id=1, source_target_pairs={{5,0},{6,1},{7,2},{4,3},{9,4},{10,5},{11,6},{8,7},{13,8},{14,9},{1... | collective-permute-start | bytes 98312 | tf_op jit(solution)/shard_map/cond/branch_1_fun/ppermute | solution.py:333
  59.0 5.5 %collective-permute-start.30 = (bf16[64,512]{1,0:T(8,128)(2,1)S(1)}, bf16[64,512]{1,0:T(8,128)(2,1)S(1)}, u32[]{:S(2)}, u32[]{:S(2)}) collective-permute-start(bf16[64,512]{1,0:T(8,128)(2,1)S(1)} %get-tuple-element.455), channel_id=1, source_target_pairs={{4,0},{8,4},{12,8},{16,12},{20,16},{24,20},{28,24},{0,28},{5,1},{9... | collective-permute-start | bytes 196616 | tf_op jit(solution)/shard_map/cond/branch_1_fun/ppermute | solution.py:334
  59.3 5.2 %collective-permute-start.31 = (bf16[64,512]{1,0:T(8,128)(2,1)S(1)}, bf16[64,512]{1,0:T(8,128)(2,1)S(1)}, u32[]{:S(2)}, u32[]{:S(2)}) collective-permute-start(bf16[64,512]{1,0:T(8,128)(2,1)S(1)} %get-tuple-element.456), channel_id=1, source_target_pairs={{1,0},{2,1},{3,2},{0,3},{5,4},{6,5},{7,6},{4,7},{9,8},{10,9},{11,1... | collective-permute-start | bytes 196616 | tf_op jit(solution)/shard_map/cond/branch_1_fun/ppermute | solution.py:332
